TPU v7x, 256 devices: a whole 4x4x8 slice. The times are simulated.
256 devices in a mesh: rep: 4 (over x_lo, core), shard: 64 (over z, y, x_hi).
Axes of the slice: x: 4 (x_hi: 2, x_lo: 2; x = x_hi * 2 + x_lo), y: 4, z: 8, core: 2. Of those that a mesh axis runs over, the one named last changes fastest.
Arguments:
- grad: float32 [128, 512, 512], P('rep', 'shard'), may hold values from -60 to 60
- momentum: bfloat16 [128, 512, 512], P('rep', 'shard'), may hold values from -6 to 6
- owners: int32 [128, 1], P('rep'), may hold values from 0 to 63, as said below
- left_roots: bfloat16 [4, 64, 2, 512, 512], P('rep', 'shard'), may hold values from -1 to 2
- right_roots: bfloat16 [4, 64, 2, 512, 512], P('rep', 'shard'), may hold values from -1 to 2
Outputs:
- momentum_next: bfloat16 [128, 512, 512], P('rep', 'shard')
- update: bfloat16 [128, 512, 512], P(None, 'shard')
Inputs may be any that keep to these rules, and one draw needn't show every extreme that they name: `owners`: within the 32 blocks of each replica part no owner is named more than 2 times, and some owner exactly 2 times.
All inputs are finite; a program needn't handle non-finite values.
Results may differ from a plain program's by a relative error of at most 0.0059.
Values may be sent and summed in bfloat16 or wider, within the bound.
No kernel may reach another device: no remote copies, remote signals or barrier semaphores. Data moves between devices by JAX's collectives and lax.ppermute only.
A program may use at most 64 MiB of HBM per device.

v0:
```python
import functools

import jax
import jax.numpy as jnp
from jax import lax
from jax.experimental import pallas as pl
from jax.experimental.pallas import tpu as pltpu
from jax.sharding import PartitionSpec as P

momentum_decay = 0.9
graft_eps = 1e-06
LANES = 128
HOPS = (36, 2)


def pack_kernel(owner_ref, token_ref, grad_ref, out_ref, index_ref, count_ref):
    owners, capacity = count_ref.shape[0], out_ref.shape[0] // count_ref.shape[0]
    blocks, _, width = grad_ref.shape
    late = lax.rem(lax.axis_index("rep"), 2) == 1
    out_ref[...] = jnp.zeros_like(out_ref)

    def clear(at, carry):
        count_ref[at] = 0
        return carry

    lax.fori_loop(0, owners, clear, 0, unroll=True)

    def place(block, carry):
        owner = jnp.where(late, token_ref[0, block], owner_ref[0, block])
        slot = count_ref[owner]
        count_ref[owner] = slot + 1
        index = owner * capacity + slot
        index_ref[block] = index
        rows = grad_ref[block]
        stacked = jnp.concatenate(
            [rows[:, at : at + LANES] for at in range(0, width, LANES)], axis=0
        )
        out_ref[index] = stacked.astype(out_ref.dtype)
        return carry

    lax.fori_loop(0, blocks, place, 0, unroll=True)


def pack(grad, owners, token, shard_count, capacity):
    blocks, rows, width = grad.shape
    stacked_rows = rows * (width // LANES)
    return pl.pallas_call(
        pack_kernel,
        out_shape=(
            jax.ShapeDtypeStruct((shard_count * capacity, stacked_rows, LANES), jnp.bfloat16),
            jax.ShapeDtypeStruct((blocks,), jnp.int32),
        ),
        in_specs=[
            pl.BlockSpec(memory_space=pltpu.SMEM),
            pl.BlockSpec(memory_space=pltpu.SMEM),
            pl.BlockSpec(memory_space=pltpu.VMEM),
        ],
        out_specs=(
            pl.BlockSpec(memory_space=pltpu.VMEM),
            pl.BlockSpec(memory_space=pltpu.SMEM),
        ),
        scratch_shapes=[pltpu.SMEM((shard_count,), jnp.int32)],
        compiler_params=pltpu.CompilerParams(vmem_limit_bytes=16 * 1024 * 1024),
    )(owners, token, grad)


def precondition_kernel(arrived_ref, left_ref, right_ref, out_ref):
    shards, slot_rows, _ = arrived_ref.shape
    capacity, order, _ = left_ref.shape
    stacked = slot_rows // capacity
    rows = order // shards
    for slot in range(capacity):
        pieces = arrived_ref[:, slot * stacked : (slot + 1) * stacked, :].astype(jnp.float32)
        block = jnp.concatenate(
            [
                pieces[:, at : at + rows, :].reshape(order, LANES)
                for at in range(0, stacked, rows)
            ],
            axis=1,
        )
        grad_norm = jnp.sqrt(jnp.sum(block * block))
        half = jnp.dot(
            left_ref[slot], block.astype(jnp.bfloat16), preferred_element_type=jnp.float32
        ).astype(jnp.bfloat16)
        precond = jnp.dot(half, right_ref[slot], preferred_element_type=jnp.float32)
        pre_norm = jnp.sqrt(jnp.sum(precond * precond) + graft_eps)
        grafted = precond * (grad_norm / pre_norm)
        out = jnp.concatenate(
            [
                grafted[:, at : at + LANES].reshape(shards, rows, LANES)
                for at in range(0, order, LANES)
            ],
            axis=1,
        )
        out_ref[:, slot * stacked : (slot + 1) * stacked, :] = out.astype(out_ref.dtype)


def precondition(arrived, left_root, right_root):
    return pl.pallas_call(
        precondition_kernel,
        out_shape=jax.ShapeDtypeStruct(arrived.shape, jnp.bfloat16),
        compiler_params=pltpu.CompilerParams(vmem_limit_bytes=40 * 1024 * 1024),
    )(arrived, left_root, right_root)


def step_kernel(index_ref, returned_ref, momentum_ref, next_ref, *update_refs):
    for part, update_ref in enumerate(update_refs):
        blocks, rows, _ = update_ref.shape

        def one(at, carry):
            block = part * blocks + at
            stacked = returned_ref[index_ref[block]].astype(jnp.float32)
            grafted = jnp.concatenate(
                [stacked[row : row + rows] for row in range(0, stacked.shape[0], rows)], axis=1
            )
            momentum_next = (
                momentum_decay * momentum_ref[block].astype(jnp.float32) + grafted
            ).astype(jnp.bfloat16)
            next_ref[block] = momentum_next
            update_ref[at] = (
                grafted + momentum_decay * momentum_next.astype(jnp.float32)
            ).astype(jnp.bfloat16)
            return carry

        lax.fori_loop(0, blocks, one, 0, unroll=True)


def step(index, returned, momentum):
    blocks, rows, width = momentum.shape
    vmem = pl.BlockSpec(memory_space=pltpu.VMEM)
    half = jax.ShapeDtypeStruct((blocks // 2, rows, width), jnp.bfloat16)
    return pl.pallas_call(
        step_kernel,
        out_shape=(jax.ShapeDtypeStruct(momentum.shape, jnp.bfloat16), half, half),
        in_specs=[pl.BlockSpec(memory_space=pltpu.SMEM), vmem, vmem],
        compiler_params=pltpu.CompilerParams(vmem_limit_bytes=16 * 1024 * 1024),
    )(index, returned, momentum)


def write_kernel(count, places, *refs):
    pieces, out_ref, sems = refs[:count], refs[-2], refs[-1]
    part = lax.axis_index("rep")
    copies = []
    for at, (flip, half) in enumerate(places):
        copies.append(
            pltpu.make_async_copy(pieces[at], out_ref.at[part ^ flip, half], sems.at[at])
        )
        copies[-1].start()
    for copy in copies:
        copy.wait()


def write(pieces, places, shape, held=()):
    anywhere = pl.BlockSpec(memory_space=pl.ANY)
    return pl.pallas_call(
        functools.partial(write_kernel, len(pieces), places),
        out_shape=jax.ShapeDtypeStruct(shape, pieces[0].dtype),
        in_specs=[pl.BlockSpec(memory_space=pltpu.VMEM)] * len(pieces) + [anywhere] * len(held),
        out_specs=anywhere,
        scratch_shapes=[pltpu.SemaphoreType.DMA((len(pieces),))],
        input_output_aliases={len(pieces): 0} if held else {},
        compiler_params=pltpu.CompilerParams(vmem_limit_bytes=8 * 1024 * 1024),
    )(*pieces, *held)


def step_and_gather(index, returned, momentum):
    swap_core = [(at, at ^ 1) for at in range(4)]
    swap_chip = [(at, at ^ 2) for at in range(4)]
    blocks, rows, width = momentum.shape
    half = blocks // 2
    next_rows, *own = step(index, returned, momentum)
    chip = [lax.ppermute(piece, "rep", swap_chip) for piece in own]
    core = [lax.ppermute(piece, "rep", swap_core) for piece in own]
    cross = [lax.ppermute(piece, "rep", swap_core) for piece in chip]
    shape = (4, 2, half, rows, width)
    out = write(own + core, ((0, 0), (0, 1), (1, 0), (1, 1)), shape)
    out = write(chip + cross, ((2, 0), (2, 1), (3, 0), (3, 1)), shape, (out,))
    return next_rows, out.reshape(4 * blocks, rows, width)


def hand_along(owners):
    shards = lax.axis_size("shard")
    for distance in HOPS:
        hops = [
            (part * shards + at, part * shards + (at + distance) % shards)
            for part in range(1, lax.axis_size("rep"), 2)
            for at in range(shards)
        ]
        owners = lax.ppermute(owners, ("rep", "shard"), hops)
    return owners


def local(grad, momentum, owners, left_roots, right_roots):
    shard_count = lax.axis_size("shard")
    capacity = left_roots.shape[2]
    owners = owners.reshape(1, -1)
    outgoing, index = pack(grad, owners, hand_along(owners), shard_count, capacity)
    stacked = outgoing.shape[1]
    outgoing = outgoing.reshape(shard_count, capacity * stacked, LANES)
    arrived = lax.all_to_all(outgoing, "shard", 0, 0, tiled=True)
    grafted = precondition(arrived, left_roots[0, 0], right_roots[0, 0])
    returned = lax.all_to_all(grafted, "shard", 0, 0, tiled=True)
    returned = returned.reshape(shard_count * capacity, stacked, LANES)
    return step_and_gather(index, returned, momentum)


def solution(mesh):
    placed = (
        P("rep", "shard", None),
        P("rep", "shard", None),
        P("rep", None),
        P("rep", "shard", None, None, None),
        P("rep", "shard", None, None, None),
    )
    return jax.shard_map(
        local,
        mesh=mesh,
        in_specs=placed,
        out_specs=(P("rep", "shard", None), P(None, "shard", None)),
        check_vma=False,
    )
```

profile of v0, /device:TPU:1, one launch (start us, length us, event | category | flops | bytes accessed | tf_op | source)
XLA Modules:
  0.0 90.3 jit_solution(4989482813359653828)
XLA Ops:
  0.6 0.0 copy-start.4
  0.6 0.6 copy-done.4
  1.3 12.3 %collective-permute-start = (s32[1,32]{1,0:T(1,128)S(1)}, s32[1,32]{1,0:T(1,128)S(1)}, u32[]{:S(2)}, u32[]{:S(2)}) collective-permute-start(s32[1,32]{1,0:T(1,128)S(1)} %bitcast.10), channel_id=1, source_target_pairs={{64,100},{65,101},{66,102},{67,103},{68,104},{69,105},{70,106},{71... | collective-permute-start | bytes 392 | tf_op jit(solution)/shard_map/ppermute | solution.py:189
  13.6 0.7 collective-permute-done
  14.3 2.3 %collective-permute-start.1 = (s32[1,32]{1,0:T(1,128)S(1)}, s32[1,32]{1,0:T(1,128)S(1)}, u32[]{:S(2)}, u32[]{:S(2)}) collective-permute-start(s32[1,32]{1,0:T(1,128)S(1)} %collective-permute-done), channel_id=1, source_target_pairs={{64,66},{65,67},{66,68},{67,69},{68,70},{69,71},{70,72},{71,73},{7... | collective-permute-start | bytes 392 | tf_op jit(solution)/shard_map/ppermute | solution.py:189
  16.6 7.0 %collective-permute-done.1.token_ref = s32[1,32]{1,0:T(1,128)S(1)} collective-permute-done((s32[1,32]{1,0:T(1,128)S(1)}, s32[1,32]{1,0:T(1,128)S(1)}, u32[]{:S(2)}, u32[]{:S(2)}) %collective-permute-start.1) | collective-permute-done | bytes 160 | tf_op jit(solution)/shard_map/ppermute | solution.py:189
  23.5 0.0 copy-start.2
  23.5 1.0 %copy-done.2 = f32[32,8,512]{2,1,0:T(8,128)S(1)} copy-done((f32[32,8,512]{2,1,0:T(8,128)S(1)}, f32[32,8,512]{2,1,0:T(8,128)}, u32[]{:S(2)}) %copy-start.2) | copy-done | bytes 524312
  24.6 1.4 %shard_map.68 = (bf16[128,32,128]{2,1,0:T(8,128)(2,1)S(1)}, s32[32]{0:T(128)S(1)}) custom-call(s32[1,32]{1,0:T(1,128)S(1)} %bitcast.11, s32[1,32]{1,0:T(1,128)S(1)} %collective-permute-done.1.token_ref, f32[32,8,512]{2,1,0:T(8,128)S(1)} %copy-done.2), custom_call_target="tpu_custom_call" | custom-call | tf_op jit(solution)/shard_map/pallas_call | solution.py:47
  26.0 0.0 copy-start
  26.0 0.0 copy-start.1
  26.0 27.3 %all_to_all.10.arrived_ref = bf16[64,64,128]{2,1,0:T(8,128)(2,1)S(1)} all-to-all(bf16[64,64,128]{2,1,0:T(8,128)(2,1)S(1)} %bitcast.7), channel_id=1, replica_groups=mesh['rep'=4,'shard'=64] {'shard'}, dimensions={0} | all-to-all | bytes 2097152 | tf_op jit(solution)/shard_map/all_to_all | solution.py:200
  53.4 0.0 copy-done
  53.4 0.0 copy-done.1
  53.4 1.8 %shard_map.69 = bf16[64,64,128]{2,1,0:T(8,128)(2,1)S(1)} custom-call(bf16[64,64,128]{2,1,0:T(8,128)(2,1)S(1)} %all_to_all.10.arrived_ref, bf16[2,512,512]{2,1,0:T(8,128)(2,1)S(1)} %bitcast.8, bf16[2,512,512]{2,1,0:T(8,128)(2,1)S(1)} %bitcast.9), custom_call_target="tpu_custom_call" | custom-call | tf_op jit(solution)/shard_map/pallas_call | solution.py:99
  55.2 0.0 copy-start.3
  55.2 26.4 %all_to_all.11 = bf16[64,64,128]{2,1,0:T(8,128)(2,1)S(1)} all-to-all(bf16[64,64,128]{2,1,0:T(8,128)(2,1)S(1)} %shard_map.69), channel_id=1, replica_groups=mesh['rep'=4,'shard'=64] {'shard'}, dimensions={0} | all-to-all | bytes 2097152 | tf_op jit(solution)/shard_map/all_to_all | solution.py:202
  81.6 0.0 copy-done.3
  81.6 1.3 %shard_map.70 = (bf16[32,8,512]{2,1,0:T(8,128)(2,1)}, bf16[16,8,512]{2,1,0:T(8,128)(2,1)S(1)}, bf16[16,8,512]{2,1,0:T(8,128)(2,1)S(1)}) custom-call(s32[32]{0:T(128)S(1)} %get-tuple-element.7.index_ref, bf16[128,32,128]{2,1,0:T(8,128)(2,1)S(1)} %bitcast.6, bf16[32,8,512]{2,1,0:T(8,128)(2,1)S(1)} %copy-done.3), custom_call_target="tpu_custom_call" | custom-call | tf_op jit(solution)/shard_map/pallas_call | solution.py:132
  82.9 0.3 collective-permute-start.2
  83.2 1.2 %collective-permute-start.3 = (bf16[16,8,512]{2,1,0:T(8,128)(2,1)S(1)}, bf16[16,8,512]{2,1,0:T(8,128)(2,1)S(1)}, u32[]{:S(2)}, u32[]{:S(2)}) collective-permute-start(bf16[16,8,512]{2,1,0:T(8,128)(2,1)S(1)} %get-tuple-element.11.refs_1_), channel_id=1, source_target_pairs={{0,128},{64,192},{128,0},{192,64},{1,129},{65,193},{129,1},{193,65... | collective-permute-start | bytes 393224 | tf_op jit(solution)/shard_map/ppermute | solution.py:172
  84.4 0.0 collective-permute-start.6
  84.4 0.5 collective-permute-start.7
  84.9 1.8 %collective-permute-done.2.refs_0_ = bf16[16,8,512]{2,1,0:T(8,128)(2,1)S(1)} collective-permute-done((bf16[16,8,512]{2,1,0:T(8,128)(2,1)S(1)}, bf16[16,8,512]{2,1,0:T(8,128)(2,1)S(1)}, u32[]{:S(2)}, u32[]{:S(2)}) %collective-permute-start.2) | collective-permute-done | bytes 131104 | tf_op jit(solution)/shard_map/ppermute | solution.py:172
  86.7 0.0 collective-permute-start.4
  86.7 1.4 %collective-permute-done.3.refs_1_ = bf16[16,8,512]{2,1,0:T(8,128)(2,1)S(1)} collective-permute-done((bf16[16,8,512]{2,1,0:T(8,128)(2,1)S(1)}, bf16[16,8,512]{2,1,0:T(8,128)(2,1)S(1)}, u32[]{:S(2)}, u32[]{:S(2)}) %collective-permute-start.3) | collective-permute-done | bytes 131104 | tf_op jit(solution)/shard_map/ppermute | solution.py:172
  88.1 0.0 collective-permute-start.5
  88.1 0.0 collective-permute-done.6.refs_2_
  88.1 0.0 collective-permute-done.7.refs_3_
  88.1 0.8 shard_map.71.refs_4_
  89.0 0.0 collective-permute-done.4.refs_2_
  89.0 0.5 collective-permute-done.5.refs_3_
  89.5 0.8 shard_map.72
Async XLA Ops:
  0.6 0.7 copy-start.4
  1.3 13.0 %collective-permute-start = (s32[1,32]{1,0:T(1,128)S(1)}, s32[1,32]{1,0:T(1,128)S(1)}, u32[]{:S(2)}, u32[]{:S(2)}) collective-permute-start(s32[1,32]{1,0:T(1,128)S(1)} %bitcast.10), channel_id=1, source_target_pairs={{64,100},{65,101},{66,102},{67,103},{68,104},{69,105},{70,106},{71... | collective-permute-start | bytes 392 | tf_op jit(solution)/shard_map/ppermute | solution.py:189
  14.3 9.3 %collective-permute-start.1 = (s32[1,32]{1,0:T(1,128)S(1)}, s32[1,32]{1,0:T(1,128)S(1)}, u32[]{:S(2)}, u32[]{:S(2)}) collective-permute-start(s32[1,32]{1,0:T(1,128)S(1)} %collective-permute-done), channel_id=1, source_target_pairs={{64,66},{65,67},{66,68},{67,69},{68,70},{69,71},{70,72},{71,73},{7... | collective-permute-start | bytes 392 | tf_op jit(solution)/shard_map/ppermute | solution.py:189
  23.5 1.0 %copy-start.2 = (f32[32,8,512]{2,1,0:T(8,128)S(1)}, f32[32,8,512]{2,1,0:T(8,128)}, u32[]{:S(2)}) copy-start(f32[32,8,512]{2,1,0:T(8,128)} %grad_ref.1) | copy-start | bytes 1572868
  26.0 27.4 %copy-start = (bf16[1,1,2,512,512]{4,3,2,1,0:T(8,128)(2,1)S(1)}, bf16[1,1,2,512,512]{4,3,2,1,0:T(8,128)(2,1)}, u32[]{:S(2)}) copy-start(bf16[1,1,2,512,512]{4,3,2,1,0:T(8,128)(2,1)} %param.8) | copy-start | bytes 3145732
  26.0 27.4 %copy-start.1 = (bf16[1,1,2,512,512]{4,3,2,1,0:T(8,128)(2,1)S(1)}, bf16[1,1,2,512,512]{4,3,2,1,0:T(8,128)(2,1)}, u32[]{:S(2)}) copy-start(bf16[1,1,2,512,512]{4,3,2,1,0:T(8,128)(2,1)} %param.9) | copy-start | bytes 3145732
  55.2 26.4 %copy-start.3 = (bf16[32,8,512]{2,1,0:T(8,128)(2,1)S(1)}, bf16[32,8,512]{2,1,0:T(8,128)(2,1)}, u32[]{:S(2)}) copy-start(bf16[32,8,512]{2,1,0:T(8,128)(2,1)} %momentum_ref.1) | copy-start | bytes 786436
  82.9 3.8 %collective-permute-start.2 = (bf16[16,8,512]{2,1,0:T(8,128)(2,1)S(1)}, bf16[16,8,512]{2,1,0:T(8,128)(2,1)S(1)}, u32[]{:S(2)}, u32[]{:S(2)}) collective-permute-start(bf16[16,8,512]{2,1,0:T(8,128)(2,1)S(1)} %get-tuple-element.10.refs_0_), channel_id=1, source_target_pairs={{0,128},{64,192},{128,0},{192,64},{1,129},{65,193},{129,1},{193,65... | collective-permute-start | bytes 393224 | tf_op jit(solution)/shard_map/ppermute | solution.py:172
  83.2 4.9 %collective-permute-start.3 = (bf16[16,8,512]{2,1,0:T(8,128)(2,1)S(1)}, bf16[16,8,512]{2,1,0:T(8,128)(2,1)S(1)}, u32[]{:S(2)}, u32[]{:S(2)}) collective-permute-start(bf16[16,8,512]{2,1,0:T(8,128)(2,1)S(1)} %get-tuple-element.11.refs_1_), channel_id=1, source_target_pairs={{0,128},{64,192},{128,0},{192,64},{1,129},{65,193},{129,1},{193,65... | collective-permute-start | bytes 393224 | tf_op jit(solution)/shard_map/ppermute | solution.py:172
  84.4 3.8 %collective-permute-start.6 = (bf16[16,8,512]{2,1,0:T(8,128)(2,1)S(1)}, bf16[16,8,512]{2,1,0:T(8,128)(2,1)S(1)}, u32[]{:S(2)}, u32[]{:S(2)}) collective-permute-start(bf16[16,8,512]{2,1,0:T(8,128)(2,1)S(1)} %get-tuple-element.10.refs_0_), channel_id=1, source_target_pairs={{0,64},{64,0},{128,192},{192,128},{1,65},{65,1},{129,193},{193,129... | collective-permute-start | bytes 393224 | tf_op jit(solution)/shard_map/ppermute | solution.py:173
  84.4 3.8 %collective-permute-start.7 = (bf16[16,8,512]{2,1,0:T(8,128)(2,1)S(1)}, bf16[16,8,512]{2,1,0:T(8,128)(2,1)S(1)}, u32[]{:S(2)}, u32[]{:S(2)}) collective-permute-start(bf16[16,8,512]{2,1,0:T(8,128)(2,1)S(1)} %get-tuple-element.11.refs_1_), channel_id=1, source_target_pairs={{0,64},{64,0},{128,192},{192,128},{1,65},{65,1},{129,193},{193,129... | collective-permute-start | bytes 393224 | tf_op jit(solution)/shard_map/ppermute | solution.py:173
  86.7 2.3 %collective-permute-start.4 = (bf16[16,8,512]{2,1,0:T(8,128)(2,1)S(1)}, bf16[16,8,512]{2,1,0:T(8,128)(2,1)S(1)}, u32[]{:S(2)}, u32[]{:S(2)}) collective-permute-start(bf16[16,8,512]{2,1,0:T(8,128)(2,1)S(1)} %collective-permute-done.2.refs_0_), channel_id=1, source_target_pairs={{0,64},{64,0},{128,192},{192,128},{1,65},{65,1},{129,193},{193,129... | collective-permute-start | bytes 393224 | tf_op jit(solution)/shard_map/ppermute | solution.py:174
  88.1 1.3 %collective-permute-start.5 = (bf16[16,8,512]{2,1,0:T(8,128)(2,1)S(1)}, bf16[16,8,512]{2,1,0:T(8,128)(2,1)S(1)}, u32[]{:S(2)}, u32[]{:S(2)}) collective-permute-start(bf16[16,8,512]{2,1,0:T(8,128)(2,1)S(1)} %collective-permute-done.3.refs_1_), channel_id=1, source_target_pairs={{0,64},{64,0},{128,192},{192,128},{1,65},{65,1},{129,193},{193,129... | collective-permute-start | bytes 393224 | tf_op jit(solution)/shard_map/ppermute | solution.py:174
where the time goes:
time: 90.6 us; the launch traced here: 90.3 us
  blocking collectives  53.7 us (59%)
  starting transfers between devices  16.5 us (18%)
  waiting for transfers between devices  11.4 us (13%)
  Pallas kernels  6.19 us (7%)
  local copies, waits for them, and re-layouts  1.71 us (2%)
    all_to_all x1, blocking collectives, local(): arrived = lax.all_to_all(outgoing, 'shard', 0, 0, tiled=True)  27.3 us
    all_to_all x1, blocking collectives, local(): returned = lax.all_to_all(grafted, 'shard', 0, 0, tiled=True)  26.4 us
    ppermute x2, starting transfers between devices, hand_along(): owners = lax.ppermute(owners, ('rep', 'shard'), hops)  14.6 us
    ppermute x2, waiting for transfers between devices, hand_along(): owners = lax.ppermute(owners, ('rep', 'shard'), hops)  7.68 us
    ppermute x2, waiting for transfers between devices, step_and_gather(): chip = [lax.ppermute(piece, 'rep', swap_chip) for piece in own]  3.24 us
    pallas_call x1, Pallas kernels, precondition(): pl.pallas_call(precondition_kernel, out_shape=jax.ShapeDtypeStruct(arrive...  1.82 us
  transfers between devices with their start and end apart: 8, of which 5 were waited for; matrix products, arithmetic and copies ran while one was open for 0% of the time, Pallas kernels for 1%

commit v1 on v0

--- a/solution.py
+++ b/solution.py
@@ -13,10 +13,9 @@
 HOPS = (36, 2)
 
 
-def pack_kernel(owner_ref, token_ref, grad_ref, out_ref, index_ref, count_ref):
+def pack_kernel(owner_ref, grad_ref, out_ref, index_ref, count_ref):
     owners, capacity = count_ref.shape[0], out_ref.shape[0] // count_ref.shape[0]
     blocks, _, width = grad_ref.shape
-    late = lax.rem(lax.axis_index("rep"), 2) == 1
     out_ref[...] = jnp.zeros_like(out_ref)
 
     def clear(at, carry):
@@ -26,7 +25,7 @@
     lax.fori_loop(0, owners, clear, 0, unroll=True)
 
     def place(block, carry):
-        owner = jnp.where(late, token_ref[0, block], owner_ref[0, block])
+        owner = owner_ref[0, block]
         slot = count_ref[owner]
         count_ref[owner] = slot + 1
         index = owner * capacity + slot
@@ -41,7 +40,7 @@
     lax.fori_loop(0, blocks, place, 0, unroll=True)
 
 
-def pack(grad, owners, token, shard_count, capacity):
+def pack(grad, owners, shard_count, capacity):
     blocks, rows, width = grad.shape
     stacked_rows = rows * (width // LANES)
     return pl.pallas_call(
@@ -51,7 +50,6 @@
             jax.ShapeDtypeStruct((blocks,), jnp.int32),
         ),
         in_specs=[
-            pl.BlockSpec(memory_space=pltpu.SMEM),
             pl.BlockSpec(memory_space=pltpu.SMEM),
             pl.BlockSpec(memory_space=pltpu.VMEM),
         ],
@@ -61,7 +59,7 @@
         ),
         scratch_shapes=[pltpu.SMEM((shard_count,), jnp.int32)],
         compiler_params=pltpu.CompilerParams(vmem_limit_bytes=16 * 1024 * 1024),
-    )(owners, token, grad)
+    )(owners, grad)
 
 
 def precondition_kernel(arrived_ref, left_ref, right_ref, out_ref):
@@ -69,22 +67,33 @@
     capacity, order, _ = left_ref.shape
     stacked = slot_rows // capacity
     rows = order // shards
-    for slot in range(capacity):
+    slots = range(capacity)
+    blocks = []
+    for slot in slots:
         pieces = arrived_ref[:, slot * stacked : (slot + 1) * stacked, :].astype(jnp.float32)
-        block = jnp.concatenate(
-            [
-                pieces[:, at : at + rows, :].reshape(order, LANES)
-                for at in range(0, stacked, rows)
-            ],
-            axis=1,
-        )
-        grad_norm = jnp.sqrt(jnp.sum(block * block))
-        half = jnp.dot(
-            left_ref[slot], block.astype(jnp.bfloat16), preferred_element_type=jnp.float32
+        blocks.append(
+            jnp.concatenate(
+                [
+                    pieces[:, at : at + rows, :].reshape(order, LANES)
+                    for at in range(0, stacked, rows)
+                ],
+                axis=1,
+            )
+        )
+    halves = [
+        jnp.dot(
+            left_ref[slot], blocks[slot].astype(jnp.bfloat16), preferred_element_type=jnp.float32
         ).astype(jnp.bfloat16)
-        precond = jnp.dot(half, right_ref[slot], preferred_element_type=jnp.float32)
-        pre_norm = jnp.sqrt(jnp.sum(precond * precond) + graft_eps)
-        grafted = precond * (grad_norm / pre_norm)
+        for slot in slots
+    ]
+    preconds = [
+        jnp.dot(halves[slot], right_ref[slot], preferred_element_type=jnp.float32)
+        for slot in slots
+    ]
+    for slot in slots:
+        grad_square = jnp.sum(blocks[slot] * blocks[slot])
+        pre_square = jnp.sum(preconds[slot] * preconds[slot]) + graft_eps
+        grafted = preconds[slot] * (jnp.sqrt(grad_square) / jnp.sqrt(pre_square))
         out = jnp.concatenate(
             [
                 grafted[:, at : at + LANES].reshape(shards, rows, LANES)
@@ -163,22 +172,33 @@
     )(*pieces, *held)
 
 
-def step_and_gather(index, returned, momentum):
+def gather_parts(own, blocks):
     swap_core = [(at, at ^ 1) for at in range(4)]
     swap_chip = [(at, at ^ 2) for at in range(4)]
-    blocks, rows, width = momentum.shape
-    half = blocks // 2
-    next_rows, *own = step(index, returned, momentum)
+    half, rows, width = own[0].shape
     chip = [lax.ppermute(piece, "rep", swap_chip) for piece in own]
     core = [lax.ppermute(piece, "rep", swap_core) for piece in own]
     cross = [lax.ppermute(piece, "rep", swap_core) for piece in chip]
     shape = (4, 2, half, rows, width)
     out = write(own + core, ((0, 0), (0, 1), (1, 0), (1, 1)), shape)
     out = write(chip + cross, ((2, 0), (2, 1), (3, 0), (3, 1)), shape, (out,))
-    return next_rows, out.reshape(4 * blocks, rows, width)
-
-
-def hand_along(owners):
+    return out.reshape(4 * blocks, rows, width)
+
+
+def swap_rows(rows):
+    return lax.all_to_all(rows, "shard", 0, 0, tiled=True)
+
+
+def early(grad, momentum, owners, left_root, right_root):
+    shards, capacity = lax.axis_size("shard"), left_root.shape[0]
+    outgoing, index = pack(grad, owners, shards, capacity)
+    stacked = outgoing.shape[1]
+    arrived = swap_rows(outgoing.reshape(shards, capacity * stacked, LANES))
+    returned = swap_rows(precondition(arrived, left_root, right_root))
+    return step(index, returned.reshape(shards * capacity, stacked, LANES), momentum)
+
+
+def late(grad, momentum, owners, left_root, right_root):
     shards = lax.axis_size("shard")
     for distance in HOPS:
         hops = [
@@ -187,21 +207,22 @@
             for at in range(shards)
         ]
         owners = lax.ppermute(owners, ("rep", "shard"), hops)
-    return owners
+    return early(grad, momentum, owners, left_root, right_root)
 
 
 def local(grad, momentum, owners, left_roots, right_roots):
-    shard_count = lax.axis_size("shard")
-    capacity = left_roots.shape[2]
-    owners = owners.reshape(1, -1)
-    outgoing, index = pack(grad, owners, hand_along(owners), shard_count, capacity)
-    stacked = outgoing.shape[1]
-    outgoing = outgoing.reshape(shard_count, capacity * stacked, LANES)
-    arrived = lax.all_to_all(outgoing, "shard", 0, 0, tiled=True)
-    grafted = precondition(arrived, left_roots[0, 0], right_roots[0, 0])
-    returned = lax.all_to_all(grafted, "shard", 0, 0, tiled=True)
-    returned = returned.reshape(shard_count * capacity, stacked, LANES)
-    return step_and_gather(index, returned, momentum)
+    odd = lax.rem(lax.axis_index("rep"), 2) == 1
+    next_rows, *own = lax.cond(
+        odd,
+        late,
+        early,
+        grad,
+        momentum,
+        owners.reshape(1, -1),
+        left_roots[0, 0],
+        right_roots[0, 0],
+    )
+    return next_rows, gather_parts(own, momentum.shape[0])
 
 
 def solution(mesh):

time: 90.6 us -> 88.7 us (0.979)
  blocking collectives: 53.7 us -> 52.4 us
  local copies, waits for them, and re-layouts: 1.71 us -> 0.67 us
    all_to_all x2, blocking collectives: 53.7 us -> 52.4 us  [swap_rows(): return lax.all_to_all(rows, 'shard', 0, 0, tiled=True)]
    unnamed x10 -> x2, local copies, waits for them, and re-layouts: 1.71 us -> 0.65 us
where the time goes in v1:
time: 88.7 us; the launch traced here: 88.5 us
  blocking collectives  52.4 us (59%)
  starting transfers between devices  16.5 us (19%)
  waiting for transfers between devices  11.4 us (13%)
  Pallas kernels  6.67 us (8%)
    all_to_all x2, blocking collectives, swap_rows(): return lax.all_to_all(rows, 'shard', 0, 0, tiled=True)  52.4 us
    ppermute x2, starting transfers between devices, late(): owners = lax.ppermute(owners, ('rep', 'shard'), hops)  14.6 us
    ppermute x2, waiting for transfers between devices, late(): owners = lax.ppermute(owners, ('rep', 'shard'), hops)  7.68 us
    ppermute x2, waiting for transfers between devices, gather_parts(): chip = [lax.ppermute(piece, 'rep', swap_chip) for piece in own]  3.24 us
    pallas_call x1, Pallas kernels, pack(): pl.pallas_call(pack_kernel, out_shape=(jax.ShapeDtypeStruct((shard_count...  1.89 us
    pallas_call x1, Pallas kernels, precondition(): pl.pallas_call(precondition_kernel, out_shape=jax.ShapeDtypeStruct(arrive...  1.8 us
  transfers between devices with their start and end apart: 8, of which 5 were waited for; matrix products, arithmetic and copies ran while one was open for 0% of the time, Pallas kernels for 1%

profile of v1, /device:TPU:1, one launch (start us, length us, event | category | flops | bytes accessed | tf_op | source)
XLA Modules:
  0.0 88.5 jit_solution(10341932150361825188)
XLA Ops:
  0.6 0.0 copy-start.6
  0.6 0.6 copy-done.6
  1.3 79.8 %conditional.1 = ((bf16[32,8,512]{2,1,0:T(8,128)(2,1)}, bf16[16,8,512]{2,1,0:T(8,128)(2,1)S(1)}, bf16[16,8,512]{2,1,0:T(8,128)(2,1)S(1)})) conditional(s32[]{:T(128)} %convert_element_type.3, (s32[1,32]{1,0:T(1,128)S(1)}, f32[32,8,512]{2,1,0:T(8,128)}, bf16[2,512,512]{2,1,0:T(8,128)(2,1)}, bf16[2,512,512]{2,1,0:T(8,128)(2,1)}, ...), branch_computations={%region_0.0_spmd, %region_1.0_spmd} | conditional | bytes 13632684 | solution.py:215
  1.3 12.3 %collective-permute-start = (s32[1,32]{1,0:T(1,128)S(1)}, s32[1,32]{1,0:T(1,128)S(1)}, u32[]{:S(2)}, u32[]{:S(2)}) collective-permute-start(s32[1,32]{1,0:T(1,128)S(1)} %get-tuple-element.27), channel_id=1, source_target_pairs={{64,100},{65,101},{66,102},{67,103},{68,104},{69,105},{70,106},{71... | collective-permute-start | bytes 392 | tf_op jit(solution)/shard_map/cond/branch_1_fun/ppermute | solution.py:209
  13.6 0.7 collective-permute-done
  14.3 2.3 %collective-permute-start.1 = (s32[1,32]{1,0:T(1,128)S(1)}, s32[1,32]{1,0:T(1,128)S(1)}, u32[]{:S(2)}, u32[]{:S(2)}) collective-permute-start(s32[1,32]{1,0:T(1,128)S(1)} %collective-permute-done), channel_id=1, source_target_pairs={{64,66},{65,67},{66,68},{67,69},{68,70},{69,71},{70,72},{71,73},{7... | collective-permute-start | bytes 392 | tf_op jit(solution)/shard_map/cond/branch_1_fun/ppermute | solution.py:209
  16.6 7.0 %collective-permute-done.1.owner_ref = s32[1,32]{1,0:T(1,128)S(1)} collective-permute-done((s32[1,32]{1,0:T(1,128)S(1)}, s32[1,32]{1,0:T(1,128)S(1)}, u32[]{:S(2)}, u32[]{:S(2)}) %collective-permute-start.1) | collective-permute-done | bytes 160 | tf_op jit(solution)/shard_map/cond/branch_1_fun/ppermute | solution.py:209
  23.6 1.9 %branch_1_fun.3 = (bf16[128,32,128]{2,1,0:T(8,128)(2,1)S(1)}, s32[32]{0:T(128)S(1)}) custom-call(s32[1,32]{1,0:T(1,128)S(1)} %collective-permute-done.1.owner_ref, f32[32,8,512]{2,1,0:T(8,128)} %get-tuple-element.28.grad_ref), custom_call_target="tpu_custom_call" | custom-call | tf_op jit(solution)/shard_map/cond/branch_1_fun/pallas_call | solution.py:46
  25.4 0.0 copy-start.1
  25.5 0.0 copy-start.3
  25.5 27.5 %all_to_all.18.arrived_ref = bf16[64,64,128]{2,1,0:T(8,128)(2,1)S(1)} all-to-all(bf16[64,64,128]{2,1,0:T(8,128)(2,1)S(1)} %bitcast.10), channel_id=1, replica_groups=mesh['rep'=4,'shard'=64] {'shard'}, dimensions={0} | all-to-all | bytes 2097152 | tf_op jit(solution)/shard_map/cond/branch_1_fun/all_to_all | solution.py:189
  53.0 0.0 copy-done.1
  53.0 0.0 copy-done.3
  53.0 1.8 %branch_1_fun.4 = bf16[64,64,128]{2,1,0:T(8,128)(2,1)S(1)} custom-call(bf16[64,64,128]{2,1,0:T(8,128)(2,1)S(1)} %all_to_all.18.arrived_ref, bf16[2,512,512]{2,1,0:T(8,128)(2,1)S(1)} %copy-done.1, bf16[2,512,512]{2,1,0:T(8,128)(2,1)S(1)} %copy-done.3), custom_call_target="tpu_custom_call" | custom-call | tf_op jit(solution)/shard_map/cond/branch_1_fun/pallas_call | solution.py:108
  54.8 0.0 copy-start.5
  54.8 24.9 %all_to_all.19 = bf16[64,64,128]{2,1,0:T(8,128)(2,1)S(1)} all-to-all(bf16[64,64,128]{2,1,0:T(8,128)(2,1)S(1)} %branch_1_fun.4), channel_id=1, replica_groups=mesh['rep'=4,'shard'=64] {'shard'}, dimensions={0} | all-to-all | bytes 2097152 | tf_op jit(solution)/shard_map/cond/branch_1_fun/all_to_all | solution.py:189
  79.7 0.0 copy-done.5
  79.7 1.3 %branch_1_fun.5 = (bf16[32,8,512]{2,1,0:T(8,128)(2,1)}, bf16[16,8,512]{2,1,0:T(8,128)(2,1)S(1)}, bf16[16,8,512]{2,1,0:T(8,128)(2,1)S(1)}) custom-call(s32[32]{0:T(128)S(1)} %get-tuple-element.29.index_ref, bf16[128,32,128]{2,1,0:T(8,128)(2,1)S(1)} %bitcast.9, bf16[32,8,512]{2,1,0:T(8,128)(2,1)S(1)} %copy-done.5), custom_call_target="tpu_custom_call" | custom-call | tf_op jit(solution)/shard_map/cond/branch_1_fun/pallas_call | solution.py:141
  81.1 0.3 collective-permute-start.2
  81.4 1.2 %collective-permute-start.3 = (bf16[16,8,512]{2,1,0:T(8,128)(2,1)S(1)}, bf16[16,8,512]{2,1,0:T(8,128)(2,1)S(1)}, u32[]{:S(2)}, u32[]{:S(2)}) collective-permute-start(bf16[16,8,512]{2,1,0:T(8,128)(2,1)S(1)} %get-tuple-element.41.refs_1_), channel_id=1, source_target_pairs={{0,128},{64,192},{128,0},{192,64},{1,129},{65,193},{129,1},{193,65... | collective-permute-start | bytes 393224 | tf_op jit(solution)/shard_map/ppermute | solution.py:179
  82.5 0.0 collective-permute-start.6
  82.5 0.5 collective-permute-start.7
  83.1 1.8 %collective-permute-done.2.refs_0_ = bf16[16,8,512]{2,1,0:T(8,128)(2,1)S(1)} collective-permute-done((bf16[16,8,512]{2,1,0:T(8,128)(2,1)S(1)}, bf16[16,8,512]{2,1,0:T(8,128)(2,1)S(1)}, u32[]{:S(2)}, u32[]{:S(2)}) %collective-permute-start.2) | collective-permute-done | bytes 131104 | tf_op jit(solution)/shard_map/ppermute | solution.py:179
  84.9 0.0 collective-permute-start.4
  84.9 1.4 %collective-permute-done.3.refs_1_ = bf16[16,8,512]{2,1,0:T(8,128)(2,1)S(1)} collective-permute-done((bf16[16,8,512]{2,1,0:T(8,128)(2,1)S(1)}, bf16[16,8,512]{2,1,0:T(8,128)(2,1)S(1)}, u32[]{:S(2)}, u32[]{:S(2)}) %collective-permute-start.3) | collective-permute-done | bytes 131104 | tf_op jit(solution)/shard_map/ppermute | solution.py:179
  86.3 0.0 collective-permute-start.5
  86.3 0.0 collective-permute-done.6.refs_2_
  86.3 0.0 collective-permute-done.7.refs_3_
  86.3 0.8 shard_map.68.refs_4_
  87.2 0.0 collective-permute-done.4.refs_2_
  87.2 0.5 collective-permute-done.5.refs_3_
  87.7 0.8 shard_map.69
Async XLA Ops:
  0.6 0.7 copy-start.6
  1.3 13.0 %collective-permute-start = (s32[1,32]{1,0:T(1,128)S(1)}, s32[1,32]{1,0:T(1,128)S(1)}, u32[]{:S(2)}, u32[]{:S(2)}) collective-permute-start(s32[1,32]{1,0:T(1,128)S(1)} %get-tuple-element.27), channel_id=1, source_target_pairs={{64,100},{65,101},{66,102},{67,103},{68,104},{69,105},{70,106},{71... | collective-permute-start | bytes 392 | tf_op jit(solution)/shard_map/cond/branch_1_fun/ppermute | solution.py:209
  14.3 9.3 %collective-permute-start.1 = (s32[1,32]{1,0:T(1,128)S(1)}, s32[1,32]{1,0:T(1,128)S(1)}, u32[]{:S(2)}, u32[]{:S(2)}) collective-permute-start(s32[1,32]{1,0:T(1,128)S(1)} %collective-permute-done), channel_id=1, source_target_pairs={{64,66},{65,67},{66,68},{67,69},{68,70},{69,71},{70,72},{71,73},{7... | collective-permute-start | bytes 392 | tf_op jit(solution)/shard_map/cond/branch_1_fun/ppermute | solution.py:209
  25.4 27.6 %copy-start.1 = (bf16[2,512,512]{2,1,0:T(8,128)(2,1)S(1)}, bf16[2,512,512]{2,1,0:T(8,128)(2,1)}, u32[]{:S(2)}) copy-start(bf16[2,512,512]{2,1,0:T(8,128)(2,1)} %get-tuple-element.31.left_ref) | copy-start | bytes 3145732 | tf_op jit(solution)/shard_map/cond
  25.5 27.5 %copy-start.3 = (bf16[2,512,512]{2,1,0:T(8,128)(2,1)S(1)}, bf16[2,512,512]{2,1,0:T(8,128)(2,1)}, u32[]{:S(2)}) copy-start(bf16[2,512,512]{2,1,0:T(8,128)(2,1)} %get-tuple-element.32.right_ref) | copy-start | bytes 3145732 | tf_op jit(solution)/shard_map/cond
  54.8 24.9 %copy-start.5 = (bf16[32,8,512]{2,1,0:T(8,128)(2,1)S(1)}, bf16[32,8,512]{2,1,0:T(8,128)(2,1)}, u32[]{:S(2)}) copy-start(bf16[32,8,512]{2,1,0:T(8,128)(2,1)} %get-tuple-element.33.momentum_ref) | copy-start | bytes 786436 | tf_op jit(solution)/shard_map/cond
  81.1 3.8 %collective-permute-start.2 = (bf16[16,8,512]{2,1,0:T(8,128)(2,1)S(1)}, bf16[16,8,512]{2,1,0:T(8,128)(2,1)S(1)}, u32[]{:S(2)}, u32[]{:S(2)}) collective-permute-start(bf16[16,8,512]{2,1,0:T(8,128)(2,1)S(1)} %get-tuple-element.40.refs_0_), channel_id=1, source_target_pairs={{0,128},{64,192},{128,0},{192,64},{1,129},{65,193},{129,1},{193,65... | collective-permute-start | bytes 393224 | tf_op jit(solution)/shard_map/ppermute | solution.py:179
  81.4 4.9 %collective-permute-start.3 = (bf16[16,8,512]{2,1,0:T(8,128)(2,1)S(1)}, bf16[16,8,512]{2,1,0:T(8,128)(2,1)S(1)}, u32[]{:S(2)}, u32[]{:S(2)}) collective-permute-start(bf16[16,8,512]{2,1,0:T(8,128)(2,1)S(1)} %get-tuple-element.41.refs_1_), channel_id=1, source_target_pairs={{0,128},{64,192},{128,0},{192,64},{1,129},{65,193},{129,1},{193,65... | collective-permute-start | bytes 393224 | tf_op jit(solution)/shard_map/ppermute | solution.py:179
  82.5 3.8 %collective-permute-start.6 = (bf16[16,8,512]{2,1,0:T(8,128)(2,1)S(1)}, bf16[16,8,512]{2,1,0:T(8,128)(2,1)S(1)}, u32[]{:S(2)}, u32[]{:S(2)}) collective-permute-start(bf16[16,8,512]{2,1,0:T(8,128)(2,1)S(1)} %get-tuple-element.40.refs_0_), channel_id=1, source_target_pairs={{0,64},{64,0},{128,192},{192,128},{1,65},{65,1},{129,193},{193,129... | collective-permute-start | bytes 393224 | tf_op jit(solution)/shard_map/ppermute | solution.py:180
  82.5 3.8 %collective-permute-start.7 = (bf16[16,8,512]{2,1,0:T(8,128)(2,1)S(1)}, bf16[16,8,512]{2,1,0:T(8,128)(2,1)S(1)}, u32[]{:S(2)}, u32[]{:S(2)}) collective-permute-start(bf16[16,8,512]{2,1,0:T(8,128)(2,1)S(1)} %get-tuple-element.41.refs_1_), channel_id=1, source_target_pairs={{0,64},{64,0},{128,192},{192,128},{1,65},{65,1},{129,193},{193,129... | collective-permute-start | bytes 393224 | tf_op jit(solution)/shard_map/ppermute | solution.py:180
  84.9 2.3 %collective-permute-start.4 = (bf16[16,8,512]{2,1,0:T(8,128)(2,1)S(1)}, bf16[16,8,512]{2,1,0:T(8,128)(2,1)S(1)}, u32[]{:S(2)}, u32[]{:S(2)}) collective-permute-start(bf16[16,8,512]{2,1,0:T(8,128)(2,1)S(1)} %collective-permute-done.2.refs_0_), channel_id=1, source_target_pairs={{0,64},{64,0},{128,192},{192,128},{1,65},{65,1},{129,193},{193,129... | collective-permute-start | bytes 393224 | tf_op jit(solution)/shard_map/ppermute | solution.py:181
  86.3 1.3 %collective-permute-start.5 = (bf16[16,8,512]{2,1,0:T(8,128)(2,1)S(1)}, bf16[16,8,512]{2,1,0:T(8,128)(2,1)S(1)}, u32[]{:S(2)}, u32[]{:S(2)}) collective-permute-start(bf16[16,8,512]{2,1,0:T(8,128)(2,1)S(1)} %collective-permute-done.3.refs_1_), channel_id=1, source_target_pairs={{0,64},{64,0},{128,192},{192,128},{1,65},{65,1},{129,193},{193,129... | collective-permute-start | bytes 393224 | tf_op jit(solution)/shard_map/ppermute | solution.py:181

commit v2 on v1

--- a/solution.py
+++ b/solution.py
@@ -11,6 +11,7 @@
 graft_eps = 1e-06
 LANES = 128
 HOPS = (36, 2)
+PIECES = (16, 16)
 
 
 def pack_kernel(owner_ref, grad_ref, out_ref, index_ref, count_ref):
@@ -113,11 +114,12 @@
 
 
 def step_kernel(index_ref, returned_ref, momentum_ref, next_ref, *update_refs):
-    for part, update_ref in enumerate(update_refs):
+    first = 0
+    for update_ref in update_refs:
         blocks, rows, _ = update_ref.shape
 
         def one(at, carry):
-            block = part * blocks + at
+            block = first + at
             stacked = returned_ref[index_ref[block]].astype(jnp.float32)
             grafted = jnp.concatenate(
                 [stacked[row : row + rows] for row in range(0, stacked.shape[0], rows)], axis=1
@@ -132,57 +134,76 @@
             return carry
 
         lax.fori_loop(0, blocks, one, 0, unroll=True)
+        first += blocks
 
 
 def step(index, returned, momentum):
-    blocks, rows, width = momentum.shape
+    _, rows, width = momentum.shape
     vmem = pl.BlockSpec(memory_space=pltpu.VMEM)
-    half = jax.ShapeDtypeStruct((blocks // 2, rows, width), jnp.bfloat16)
+    pieces = [jax.ShapeDtypeStruct((count, rows, width), jnp.bfloat16) for count in PIECES]
     return pl.pallas_call(
         step_kernel,
-        out_shape=(jax.ShapeDtypeStruct(momentum.shape, jnp.bfloat16), half, half),
+        out_shape=(jax.ShapeDtypeStruct(momentum.shape, jnp.bfloat16), *pieces),
         in_specs=[pl.BlockSpec(memory_space=pltpu.SMEM), vmem, vmem],
         compiler_params=pltpu.CompilerParams(vmem_limit_bytes=16 * 1024 * 1024),
     )(index, returned, momentum)
 
 
-def write_kernel(count, places, *refs):
-    pieces, out_ref, sems = refs[:count], refs[-2], refs[-1]
+def write_kernel(places, *refs):
+    count = len(places)
+    pieces, sems = refs[:count], refs[-1]
     part = lax.axis_index("rep")
+    whole = len(refs) == count + 4
+    out_ref = refs[-3] if whole else refs[-2]
     copies = []
-    for at, (flip, half) in enumerate(places):
+    for at, (flip, first) in enumerate(places):
+        run = pl.ds(first, pieces[at].shape[0])
         copies.append(
-            pltpu.make_async_copy(pieces[at], out_ref.at[part ^ flip, half], sems.at[at])
-        )
-        copies[-1].start()
+            pltpu.make_async_copy(pieces[at], out_ref.at[part ^ flip, run], sems.at[at])
+        )
+    if whole:
+        copies.append(pltpu.make_async_copy(refs[count], refs[-2], sems.at[count]))
+    for copy in copies:
+        copy.start()
     for copy in copies:
         copy.wait()
 
 
-def write(pieces, places, shape, held=()):
+def write(pieces, places, shape, held=None, whole=None):
     anywhere = pl.BlockSpec(memory_space=pl.ANY)
-    return pl.pallas_call(
-        functools.partial(write_kernel, len(pieces), places),
-        out_shape=jax.ShapeDtypeStruct(shape, pieces[0].dtype),
-        in_specs=[pl.BlockSpec(memory_space=pltpu.VMEM)] * len(pieces) + [anywhere] * len(held),
-        out_specs=anywhere,
-        scratch_shapes=[pltpu.SemaphoreType.DMA((len(pieces),))],
-        input_output_aliases={len(pieces): 0} if held else {},
+    vmem = pl.BlockSpec(memory_space=pltpu.VMEM)
+    operands, in_specs = list(pieces), [vmem] * len(pieces)
+    out_shape, aliases = [jax.ShapeDtypeStruct(shape, pieces[0].dtype)], {}
+    if whole is not None:
+        operands, in_specs = operands + [whole], in_specs + [vmem]
+        out_shape.append(jax.ShapeDtypeStruct(whole.shape, whole.dtype))
+    if held is not None:
+        aliases = {len(operands): 0}
+        operands, in_specs = operands + [held], in_specs + [anywhere]
+    return pl.pallas_call(
+        functools.partial(write_kernel, places),
+        out_shape=out_shape,
+        in_specs=in_specs,
+        out_specs=[anywhere] * len(out_shape),
+        scratch_shapes=[pltpu.SemaphoreType.DMA((len(pieces) + 1,))],
+        input_output_aliases=aliases,
         compiler_params=pltpu.CompilerParams(vmem_limit_bytes=8 * 1024 * 1024),
-    )(*pieces, *held)
-
-
-def gather_parts(own, blocks):
+    )(*operands)
+
+
+def gather_parts(next_rows, own):
     swap_core = [(at, at ^ 1) for at in range(4)]
     swap_chip = [(at, at ^ 2) for at in range(4)]
-    half, rows, width = own[0].shape
     chip = [lax.ppermute(piece, "rep", swap_chip) for piece in own]
     core = [lax.ppermute(piece, "rep", swap_core) for piece in own]
     cross = [lax.ppermute(piece, "rep", swap_core) for piece in chip]
-    shape = (4, 2, half, rows, width)
-    out = write(own + core, ((0, 0), (0, 1), (1, 0), (1, 1)), shape)
-    out = write(chip + cross, ((2, 0), (2, 1), (3, 0), (3, 1)), shape, (out,))
-    return out.reshape(4 * blocks, rows, width)
+    blocks, rows, width = next_rows.shape
+    shape = (4, blocks, rows, width)
+    at = (0, PIECES[0])
+    places = [tuple((flip, first) for flip in flips for first in at) for flips in ((0, 1), (2, 3))]
+    out, next_rows = write(own + core, places[0], shape, whole=next_rows)
+    (out,) = write(chip + cross, places[1], shape, held=out)
+    return next_rows, out.reshape(4 * blocks, rows, width)
 
 
 def swap_rows(rows):
@@ -222,7 +243,7 @@
         left_roots[0, 0],
         right_roots[0, 0],
     )
-    return next_rows, gather_parts(own, momentum.shape[0])
+    return gather_parts(next_rows, own)
 
 
 def solution(mesh):

time: 88.7 us -> 88.2 us (level)
  no operation moved by 1% of the time
where the time goes in v2:
time: 88.2 us; the launch traced here: 87.9 us
  blocking collectives  52.4 us (59%)
  starting transfers between devices  16.6 us (19%)
  waiting for transfers between devices  11.3 us (13%)
  Pallas kernels  6.14 us (7%)
    all_to_all x2, blocking collectives, swap_rows(): return lax.all_to_all(rows, 'shard', 0, 0, tiled=True)  52.4 us
    ppermute x2, starting transfers between devices, late(): owners = lax.ppermute(owners, ('rep', 'shard'), hops)  14.6 us
    ppermute x2, waiting for transfers between devices, late(): owners = lax.ppermute(owners, ('rep', 'shard'), hops)  7.68 us
    ppermute x2, waiting for transfers between devices, gather_parts(): chip = [lax.ppermute(piece, 'rep', swap_chip) for piece in own]  3.24 us
    pallas_call x1, Pallas kernels, pack(): pl.pallas_call(pack_kernel, out_shape=(jax.ShapeDtypeStruct((shard_count...  1.89 us
    pallas_call x1, Pallas kernels, precondition(): pl.pallas_call(precondition_kernel, out_shape=jax.ShapeDtypeStruct(arrive...  1.8 us
  transfers between devices with their start and end apart: 8, of which 5 were waited for; matrix products, arithmetic and copies ran while one was open for 0% of the time, Pallas kernels for 1%

profile of v2, /device:TPU:1, one launch (start us, length us, event | category | flops | bytes accessed | tf_op | source)
XLA Modules:
  0.0 87.9 jit_solution(15231178438144560803)
XLA Ops:
  0.6 0.0 copy-start.6
  0.6 0.6 copy-done.6
  1.3 79.2 %conditional.1 = ((bf16[32,8,512]{2,1,0:T(8,128)(2,1)S(1)}, bf16[16,8,512]{2,1,0:T(8,128)(2,1)S(1)}, bf16[16,8,512]{2,1,0:T(8,128)(2,1)S(1)})) conditional(s32[]{:T(128)} %convert_element_type.3, (s32[1,32]{1,0:T(1,128)S(1)}, f32[32,8,512]{2,1,0:T(8,128)}, bf16[2,512,512]{2,1,0:T(8,128)(2,1)}, bf16[2,512,512]{2,1,0:T(8,128)(2,1)}, ...), branch_computations={%region_0.0_spmd, %region_1.0_spmd} | conditional | bytes 13632684 | solution.py:236
  1.3 12.3 %collective-permute-start = (s32[1,32]{1,0:T(1,128)S(1)}, s32[1,32]{1,0:T(1,128)S(1)}, u32[]{:S(2)}, u32[]{:S(2)}) collective-permute-start(s32[1,32]{1,0:T(1,128)S(1)} %get-tuple-element.27), channel_id=1, source_target_pairs={{64,100},{65,101},{66,102},{67,103},{68,104},{69,105},{70,106},{71... | collective-permute-start | bytes 392 | tf_op jit(solution)/shard_map/cond/branch_1_fun/ppermute | solution.py:230
  13.6 0.7 collective-permute-done
  14.3 2.3 %collective-permute-start.1 = (s32[1,32]{1,0:T(1,128)S(1)}, s32[1,32]{1,0:T(1,128)S(1)}, u32[]{:S(2)}, u32[]{:S(2)}) collective-permute-start(s32[1,32]{1,0:T(1,128)S(1)} %collective-permute-done), channel_id=1, source_target_pairs={{64,66},{65,67},{66,68},{67,69},{68,70},{69,71},{70,72},{71,73},{7... | collective-permute-start | bytes 392 | tf_op jit(solution)/shard_map/cond/branch_1_fun/ppermute | solution.py:230
  16.6 7.0 %collective-permute-done.1.owner_ref = s32[1,32]{1,0:T(1,128)S(1)} collective-permute-done((s32[1,32]{1,0:T(1,128)S(1)}, s32[1,32]{1,0:T(1,128)S(1)}, u32[]{:S(2)}, u32[]{:S(2)}) %collective-permute-start.1) | collective-permute-done | bytes 160 | tf_op jit(solution)/shard_map/cond/branch_1_fun/ppermute | solution.py:230
  23.6 1.9 %branch_1_fun.3 = (bf16[128,32,128]{2,1,0:T(8,128)(2,1)S(1)}, s32[32]{0:T(128)S(1)}) custom-call(s32[1,32]{1,0:T(1,128)S(1)} %collective-permute-done.1.owner_ref, f32[32,8,512]{2,1,0:T(8,128)} %get-tuple-element.28.grad_ref), custom_call_target="tpu_custom_call" | custom-call | tf_op jit(solution)/shard_map/cond/branch_1_fun/pallas_call | solution.py:47
  25.4 0.0 copy-start.1
  25.5 0.0 copy-start.3
  25.5 27.5 %all_to_all.18.arrived_ref = bf16[64,64,128]{2,1,0:T(8,128)(2,1)S(1)} all-to-all(bf16[64,64,128]{2,1,0:T(8,128)(2,1)S(1)} %bitcast.10), channel_id=1, replica_groups=mesh['rep'=4,'shard'=64] {'shard'}, dimensions={0} | all-to-all | bytes 2097152 | tf_op jit(solution)/shard_map/cond/branch_1_fun/all_to_all | solution.py:210
  53.0 0.0 copy-done.1
  53.0 0.0 copy-done.3
  53.0 1.8 %branch_1_fun.4 = bf16[64,64,128]{2,1,0:T(8,128)(2,1)S(1)} custom-call(bf16[64,64,128]{2,1,0:T(8,128)(2,1)S(1)} %all_to_all.18.arrived_ref, bf16[2,512,512]{2,1,0:T(8,128)(2,1)S(1)} %copy-done.1, bf16[2,512,512]{2,1,0:T(8,128)(2,1)S(1)} %copy-done.3), custom_call_target="tpu_custom_call" | custom-call | tf_op jit(solution)/shard_map/cond/branch_1_fun/pallas_call | solution.py:109
  54.8 0.0 copy-start.5
  54.8 24.9 %all_to_all.19 = bf16[64,64,128]{2,1,0:T(8,128)(2,1)S(1)} all-to-all(bf16[64,64,128]{2,1,0:T(8,128)(2,1)S(1)} %branch_1_fun.4), channel_id=1, replica_groups=mesh['rep'=4,'shard'=64] {'shard'}, dimensions={0} | all-to-all | bytes 2097152 | tf_op jit(solution)/shard_map/cond/branch_1_fun/all_to_all | solution.py:210
  79.7 0.0 copy-done.5
  79.7 0.7 branch_1_fun.5
  80.4 0.4 collective-permute-start.4
  80.8 1.2 %collective-permute-start.5 = (bf16[16,8,512]{2,1,0:T(8,128)(2,1)S(1)}, bf16[16,8,512]{2,1,0:T(8,128)(2,1)S(1)}, u32[]{:S(2)}, u32[]{:S(2)}) collective-permute-start(bf16[16,8,512]{2,1,0:T(8,128)(2,1)S(1)} %get-tuple-element.42.refs_1_), channel_id=1, source_target_pairs={{0,128},{64,192},{128,0},{192,64},{1,129},{65,193},{129,1},{193,65... | collective-permute-start | bytes 393224 | tf_op jit(solution)/shard_map/ppermute | solution.py:197
  82.0 0.0 collective-permute-start.2
  82.0 0.5 collective-permute-start.3
  82.5 1.8 %collective-permute-done.4.refs_0_ = bf16[16,8,512]{2,1,0:T(8,128)(2,1)S(1)} collective-permute-done((bf16[16,8,512]{2,1,0:T(8,128)(2,1)S(1)}, bf16[16,8,512]{2,1,0:T(8,128)(2,1)S(1)}, u32[]{:S(2)}, u32[]{:S(2)}) %collective-permute-start.4) | collective-permute-done | bytes 131104 | tf_op jit(solution)/shard_map/ppermute | solution.py:197
  84.4 0.0 collective-permute-start.6
  84.4 1.4 %collective-permute-done.5.refs_1_ = bf16[16,8,512]{2,1,0:T(8,128)(2,1)S(1)} collective-permute-done((bf16[16,8,512]{2,1,0:T(8,128)(2,1)S(1)}, bf16[16,8,512]{2,1,0:T(8,128)(2,1)S(1)}, u32[]{:S(2)}, u32[]{:S(2)}) %collective-permute-start.5) | collective-permute-done | bytes 131104 | tf_op jit(solution)/shard_map/ppermute | solution.py:197
  85.8 0.0 collective-permute-start.7
  85.8 0.0 collective-permute-done.2.refs_2_
  85.8 0.0 collective-permute-done.3.refs_3_
  85.8 0.9 %shard_map.68 = (bf16[4,32,8,512]{3,2,1,0:T(8,128)(2,1)}, bf16[32,8,512]{2,1,0:T(8,128)(2,1)}) custom-call(bf16[16,8,512]{2,1,0:T(8,128)(2,1)S(1)} %get-tuple-element.41.refs_0_, bf16[16,8,512]{2,1,0:T(8,128)(2,1)S(1)} %get-tuple-element.42.refs_1_, bf16[16,8,512]{2,1,0:T(8,128)(2,1)S(1)} %collective-permute-done.2.refs_2_, ...), custom_call_target="tpu_custom_call" | custom-call | tf_op jit(solution)/shard_map/pallas_call | solution.py:183
  86.7 0.0 collective-permute-done.6.refs_2_
  86.7 0.4 collective-permute-done.7.refs_3_
  87.1 0.8 shard_map.69
Async XLA Ops:
  0.6 0.7 copy-start.6
  1.3 13.0 %collective-permute-start = (s32[1,32]{1,0:T(1,128)S(1)}, s32[1,32]{1,0:T(1,128)S(1)}, u32[]{:S(2)}, u32[]{:S(2)}) collective-permute-start(s32[1,32]{1,0:T(1,128)S(1)} %get-tuple-element.27), channel_id=1, source_target_pairs={{64,100},{65,101},{66,102},{67,103},{68,104},{69,105},{70,106},{71... | collective-permute-start | bytes 392 | tf_op jit(solution)/shard_map/cond/branch_1_fun/ppermute | solution.py:230
  14.3 9.3 %collective-permute-start.1 = (s32[1,32]{1,0:T(1,128)S(1)}, s32[1,32]{1,0:T(1,128)S(1)}, u32[]{:S(2)}, u32[]{:S(2)}) collective-permute-start(s32[1,32]{1,0:T(1,128)S(1)} %collective-permute-done), channel_id=1, source_target_pairs={{64,66},{65,67},{66,68},{67,69},{68,70},{69,71},{70,72},{71,73},{7... | collective-permute-start | bytes 392 | tf_op jit(solution)/shard_map/cond/branch_1_fun/ppermute | solution.py:230
  25.4 27.6 %copy-start.1 = (bf16[2,512,512]{2,1,0:T(8,128)(2,1)S(1)}, bf16[2,512,512]{2,1,0:T(8,128)(2,1)}, u32[]{:S(2)}) copy-start(bf16[2,512,512]{2,1,0:T(8,128)(2,1)} %get-tuple-element.31.left_ref) | copy-start | bytes 3145732 | tf_op jit(solution)/shard_map/cond
  25.5 27.5 %copy-start.3 = (bf16[2,512,512]{2,1,0:T(8,128)(2,1)S(1)}, bf16[2,512,512]{2,1,0:T(8,128)(2,1)}, u32[]{:S(2)}) copy-start(bf16[2,512,512]{2,1,0:T(8,128)(2,1)} %get-tuple-element.32.right_ref) | copy-start | bytes 3145732 | tf_op jit(solution)/shard_map/cond
  54.8 24.9 %copy-start.5 = (bf16[32,8,512]{2,1,0:T(8,128)(2,1)S(1)}, bf16[32,8,512]{2,1,0:T(8,128)(2,1)}, u32[]{:S(2)}) copy-start(bf16[32,8,512]{2,1,0:T(8,128)(2,1)} %get-tuple-element.33.momentum_ref) | copy-start | bytes 786436 | tf_op jit(solution)/shard_map/cond
  80.4 3.9 %collective-permute-start.4 = (bf16[16,8,512]{2,1,0:T(8,128)(2,1)S(1)}, bf16[16,8,512]{2,1,0:T(8,128)(2,1)S(1)}, u32[]{:S(2)}, u32[]{:S(2)}) collective-permute-start(bf16[16,8,512]{2,1,0:T(8,128)(2,1)S(1)} %get-tuple-element.41.refs_0_), channel_id=1, source_target_pairs={{0,128},{64,192},{128,0},{192,64},{1,129},{65,193},{129,1},{193,65... | collective-permute-start | bytes 393224 | tf_op jit(solution)/shard_map/ppermute | solution.py:197
  80.8 4.9 %collective-permute-start.5 = (bf16[16,8,512]{2,1,0:T(8,128)(2,1)S(1)}, bf16[16,8,512]{2,1,0:T(8,128)(2,1)S(1)}, u32[]{:S(2)}, u32[]{:S(2)}) collective-permute-start(bf16[16,8,512]{2,1,0:T(8,128)(2,1)S(1)} %get-tuple-element.42.refs_1_), channel_id=1, source_target_pairs={{0,128},{64,192},{128,0},{192,64},{1,129},{65,193},{129,1},{193,65... | collective-permute-start | bytes 393224 | tf_op jit(solution)/shard_map/ppermute | solution.py:197
  82.0 3.8 %collective-permute-start.2 = (bf16[16,8,512]{2,1,0:T(8,128)(2,1)S(1)}, bf16[16,8,512]{2,1,0:T(8,128)(2,1)S(1)}, u32[]{:S(2)}, u32[]{:S(2)}) collective-permute-start(bf16[16,8,512]{2,1,0:T(8,128)(2,1)S(1)} %get-tuple-element.41.refs_0_), channel_id=1, source_target_pairs={{0,64},{64,0},{128,192},{192,128},{1,65},{65,1},{129,193},{193,129... | collective-permute-start | bytes 393224 | tf_op jit(solution)/shard_map/ppermute | solution.py:198
  82.0 3.8 %collective-permute-start.3 = (bf16[16,8,512]{2,1,0:T(8,128)(2,1)S(1)}, bf16[16,8,512]{2,1,0:T(8,128)(2,1)S(1)}, u32[]{:S(2)}, u32[]{:S(2)}) collective-permute-start(bf16[16,8,512]{2,1,0:T(8,128)(2,1)S(1)} %get-tuple-element.42.refs_1_), channel_id=1, source_target_pairs={{0,64},{64,0},{128,192},{192,128},{1,65},{65,1},{129,193},{193,129... | collective-permute-start | bytes 393224 | tf_op jit(solution)/shard_map/ppermute | solution.py:198
  84.4 2.4 %collective-permute-start.6 = (bf16[16,8,512]{2,1,0:T(8,128)(2,1)S(1)}, bf16[16,8,512]{2,1,0:T(8,128)(2,1)S(1)}, u32[]{:S(2)}, u32[]{:S(2)}) collective-permute-start(bf16[16,8,512]{2,1,0:T(8,128)(2,1)S(1)} %collective-permute-done.4.refs_0_), channel_id=1, source_target_pairs={{0,64},{64,0},{128,192},{192,128},{1,65},{65,1},{129,193},{193,129... | collective-permute-start | bytes 393224 | tf_op jit(solution)/shard_map/ppermute | solution.py:199
  85.8 1.3 %collective-permute-start.7 = (bf16[16,8,512]{2,1,0:T(8,128)(2,1)S(1)}, bf16[16,8,512]{2,1,0:T(8,128)(2,1)S(1)}, u32[]{:S(2)}, u32[]{:S(2)}) collective-permute-start(bf16[16,8,512]{2,1,0:T(8,128)(2,1)S(1)} %collective-permute-done.5.refs_1_), channel_id=1, source_target_pairs={{0,64},{64,0},{128,192},{192,128},{1,65},{65,1},{129,193},{193,129... | collective-permute-start | bytes 393224 | tf_op jit(solution)/shard_map/ppermute | solution.py:199

commit v3 on v2

--- a/solution.py
+++ b/solution.py
@@ -199,10 +199,13 @@
     cross = [lax.ppermute(piece, "rep", swap_core) for piece in chip]
     blocks, rows, width = next_rows.shape
     shape = (4, blocks, rows, width)
-    at = (0, PIECES[0])
-    places = [tuple((flip, first) for flip in flips for first in at) for flips in ((0, 1), (2, 3))]
-    out, next_rows = write(own + core, places[0], shape, whole=next_rows)
-    (out,) = write(chip + cross, places[1], shape, held=out)
+    starts = [sum(PIECES[:at]) for at in range(len(PIECES))]
+    last = starts[-1]
+    places = [(flip, first) for flip in (0, 1, 2) for first in starts]
+    places += [(3, first) for first in starts[:-1]]
+    pieces = own + core + chip + cross[:-1]
+    out, next_rows = write(pieces, tuple(places), shape, whole=next_rows)
+    (out,) = write(cross[-1:], ((3, last),), shape, held=out)
     return next_rows, out.reshape(4 * blocks, rows, width)
 
 

time: 88.2 us -> 88.1 us (level)
  no operation moved by 1% of the time
where the time goes in v3:
time: 88.1 us; the launch traced here: 87.8 us
  blocking collectives  52.4 us (59%)
  starting transfers between devices  16.6 us (19%)
  waiting for transfers between devices  11.2 us (13%)
  Pallas kernels  6.15 us (7%)
    all_to_all x2, blocking collectives, swap_rows(): return lax.all_to_all(rows, 'shard', 0, 0, tiled=True)  52.4 us
    ppermute x2, starting transfers between devices, late(): owners = lax.ppermute(owners, ('rep', 'shard'), hops)  14.6 us
    ppermute x2, waiting for transfers between devices, late(): owners = lax.ppermute(owners, ('rep', 'shard'), hops)  7.68 us
    ppermute x2, waiting for transfers between devices, gather_parts(): chip = [lax.ppermute(piece, 'rep', swap_chip) for piece in own]  3.24 us
    pallas_call x1, Pallas kernels, pack(): pl.pallas_call(pack_kernel, out_shape=(jax.ShapeDtypeStruct((shard_count...  1.89 us
    pallas_call x1, Pallas kernels, precondition(): pl.pallas_call(precondition_kernel, out_shape=jax.ShapeDtypeStruct(arrive...  1.8 us
  transfers between devices with their start and end apart: 8, of which 5 were waited for; matrix products, arithmetic and copies ran while one was open for 0% of the time, Pallas kernels for 1%

profile of v3, /device:TPU:1, one launch (start us, length us, event | category | flops | bytes accessed | tf_op | source)
XLA Modules:
  0.0 87.8 jit_solution(6215222752931701412)
XLA Ops:
  0.6 0.0 copy-start.6
  0.6 0.6 copy-done.6
  1.3 79.2 %conditional.1 = ((bf16[32,8,512]{2,1,0:T(8,128)(2,1)S(1)}, bf16[16,8,512]{2,1,0:T(8,128)(2,1)S(1)}, bf16[16,8,512]{2,1,0:T(8,128)(2,1)S(1)})) conditional(s32[]{:T(128)} %convert_element_type.3, (s32[1,32]{1,0:T(1,128)S(1)}, f32[32,8,512]{2,1,0:T(8,128)}, bf16[2,512,512]{2,1,0:T(8,128)(2,1)}, bf16[2,512,512]{2,1,0:T(8,128)(2,1)}, ...), branch_computations={%region_0.0_spmd, %region_1.0_spmd} | conditional | bytes 13632684 | solution.py:239
  1.3 12.3 %collective-permute-start = (s32[1,32]{1,0:T(1,128)S(1)}, s32[1,32]{1,0:T(1,128)S(1)}, u32[]{:S(2)}, u32[]{:S(2)}) collective-permute-start(s32[1,32]{1,0:T(1,128)S(1)} %get-tuple-element.27), channel_id=1, source_target_pairs={{64,100},{65,101},{66,102},{67,103},{68,104},{69,105},{70,106},{71... | collective-permute-start | bytes 392 | tf_op jit(solution)/shard_map/cond/branch_1_fun/ppermute | solution.py:233
  13.6 0.7 collective-permute-done
  14.3 2.3 %collective-permute-start.1 = (s32[1,32]{1,0:T(1,128)S(1)}, s32[1,32]{1,0:T(1,128)S(1)}, u32[]{:S(2)}, u32[]{:S(2)}) collective-permute-start(s32[1,32]{1,0:T(1,128)S(1)} %collective-permute-done), channel_id=1, source_target_pairs={{64,66},{65,67},{66,68},{67,69},{68,70},{69,71},{70,72},{71,73},{7... | collective-permute-start | bytes 392 | tf_op jit(solution)/shard_map/cond/branch_1_fun/ppermute | solution.py:233
  16.6 7.0 %collective-permute-done.1.owner_ref = s32[1,32]{1,0:T(1,128)S(1)} collective-permute-done((s32[1,32]{1,0:T(1,128)S(1)}, s32[1,32]{1,0:T(1,128)S(1)}, u32[]{:S(2)}, u32[]{:S(2)}) %collective-permute-start.1) | collective-permute-done | bytes 160 | tf_op jit(solution)/shard_map/cond/branch_1_fun/ppermute | solution.py:233
  23.6 1.9 %branch_1_fun.3 = (bf16[128,32,128]{2,1,0:T(8,128)(2,1)S(1)}, s32[32]{0:T(128)S(1)}) custom-call(s32[1,32]{1,0:T(1,128)S(1)} %collective-permute-done.1.owner_ref, f32[32,8,512]{2,1,0:T(8,128)} %get-tuple-element.28.grad_ref), custom_call_target="tpu_custom_call" | custom-call | tf_op jit(solution)/shard_map/cond/branch_1_fun/pallas_call | solution.py:47
  25.4 0.0 copy-start.1
  25.5 0.0 copy-start.3
  25.5 27.5 %all_to_all.18.arrived_ref = bf16[64,64,128]{2,1,0:T(8,128)(2,1)S(1)} all-to-all(bf16[64,64,128]{2,1,0:T(8,128)(2,1)S(1)} %bitcast.10), channel_id=1, replica_groups=mesh['rep'=4,'shard'=64] {'shard'}, dimensions={0} | all-to-all | bytes 2097152 | tf_op jit(solution)/shard_map/cond/branch_1_fun/all_to_all | solution.py:213
  53.0 0.0 copy-done.1
  53.0 0.0 copy-done.3
  53.0 1.8 %branch_1_fun.4 = bf16[64,64,128]{2,1,0:T(8,128)(2,1)S(1)} custom-call(bf16[64,64,128]{2,1,0:T(8,128)(2,1)S(1)} %all_to_all.18.arrived_ref, bf16[2,512,512]{2,1,0:T(8,128)(2,1)S(1)} %copy-done.1, bf16[2,512,512]{2,1,0:T(8,128)(2,1)S(1)} %copy-done.3), custom_call_target="tpu_custom_call" | custom-call | tf_op jit(solution)/shard_map/cond/branch_1_fun/pallas_call | solution.py:109
  54.8 0.0 copy-start.5
  54.8 24.9 %all_to_all.19 = bf16[64,64,128]{2,1,0:T(8,128)(2,1)S(1)} all-to-all(bf16[64,64,128]{2,1,0:T(8,128)(2,1)S(1)} %branch_1_fun.4), channel_id=1, replica_groups=mesh['rep'=4,'shard'=64] {'shard'}, dimensions={0} | all-to-all | bytes 2097152 | tf_op jit(solution)/shard_map/cond/branch_1_fun/all_to_all | solution.py:213
  79.7 0.0 copy-done.5
  79.7 0.7 branch_1_fun.5
  80.4 0.4 collective-permute-start.4
  80.8 1.2 %collective-permute-start.5 = (bf16[16,8,512]{2,1,0:T(8,128)(2,1)S(1)}, bf16[16,8,512]{2,1,0:T(8,128)(2,1)S(1)}, u32[]{:S(2)}, u32[]{:S(2)}) collective-permute-start(bf16[16,8,512]{2,1,0:T(8,128)(2,1)S(1)} %get-tuple-element.42.refs_1_), channel_id=1, source_target_pairs={{0,128},{64,192},{128,0},{192,64},{1,129},{65,193},{129,1},{193,65... | collective-permute-start | bytes 393224 | tf_op jit(solution)/shard_map/ppermute | solution.py:197
  82.0 0.0 collective-permute-start.2
  82.0 0.5 collective-permute-start.3
  82.5 1.8 %collective-permute-done.4.refs_4_ = bf16[16,8,512]{2,1,0:T(8,128)(2,1)S(1)} collective-permute-done((bf16[16,8,512]{2,1,0:T(8,128)(2,1)S(1)}, bf16[16,8,512]{2,1,0:T(8,128)(2,1)S(1)}, u32[]{:S(2)}, u32[]{:S(2)}) %collective-permute-start.4) | collective-permute-done | bytes 131104 | tf_op jit(solution)/shard_map/ppermute | solution.py:197
  84.4 0.0 collective-permute-start.6
  84.4 1.4 %collective-permute-done.5.refs_5_ = bf16[16,8,512]{2,1,0:T(8,128)(2,1)S(1)} collective-permute-done((bf16[16,8,512]{2,1,0:T(8,128)(2,1)S(1)}, bf16[16,8,512]{2,1,0:T(8,128)(2,1)S(1)}, u32[]{:S(2)}, u32[]{:S(2)}) %collective-permute-start.5) | collective-permute-done | bytes 131104 | tf_op jit(solution)/shard_map/ppermute | solution.py:197
  85.8 0.0 collective-permute-start.7
  85.8 0.0 collective-permute-done.2.refs_2_
  85.8 0.0 collective-permute-done.3.refs_3_
  85.8 0.0 collective-permute-done.6.refs_6_
  85.8 1.1 %shard_map.68 = (bf16[4,32,8,512]{3,2,1,0:T(8,128)(2,1)}, bf16[32,8,512]{2,1,0:T(8,128)(2,1)}) custom-call(bf16[16,8,512]{2,1,0:T(8,128)(2,1)S(1)} %get-tuple-element.41.refs_0_, bf16[16,8,512]{2,1,0:T(8,128)(2,1)S(1)} %get-tuple-element.42.refs_1_, bf16[16,8,512]{2,1,0:T(8,128)(2,1)S(1)} %collective-permute-done.2.refs_2_, ...), custom_call_target="tpu_custom_call" | custom-call | tf_op jit(solution)/shard_map/pallas_call | solution.py:183
  86.9 0.2 collective-permute-done.7.refs_0_
  87.1 0.7 shard_map.69
Async XLA Ops:
  0.6 0.7 copy-start.6
  1.3 13.0 %collective-permute-start = (s32[1,32]{1,0:T(1,128)S(1)}, s32[1,32]{1,0:T(1,128)S(1)}, u32[]{:S(2)}, u32[]{:S(2)}) collective-permute-start(s32[1,32]{1,0:T(1,128)S(1)} %get-tuple-element.27), channel_id=1, source_target_pairs={{64,100},{65,101},{66,102},{67,103},{68,104},{69,105},{70,106},{71... | collective-permute-start | bytes 392 | tf_op jit(solution)/shard_map/cond/branch_1_fun/ppermute | solution.py:233
  14.3 9.3 %collective-permute-start.1 = (s32[1,32]{1,0:T(1,128)S(1)}, s32[1,32]{1,0:T(1,128)S(1)}, u32[]{:S(2)}, u32[]{:S(2)}) collective-permute-start(s32[1,32]{1,0:T(1,128)S(1)} %collective-permute-done), channel_id=1, source_target_pairs={{64,66},{65,67},{66,68},{67,69},{68,70},{69,71},{70,72},{71,73},{7... | collective-permute-start | bytes 392 | tf_op jit(solution)/shard_map/cond/branch_1_fun/ppermute | solution.py:233
  25.4 27.6 %copy-start.1 = (bf16[2,512,512]{2,1,0:T(8,128)(2,1)S(1)}, bf16[2,512,512]{2,1,0:T(8,128)(2,1)}, u32[]{:S(2)}) copy-start(bf16[2,512,512]{2,1,0:T(8,128)(2,1)} %get-tuple-element.31.left_ref) | copy-start | bytes 3145732 | tf_op jit(solution)/shard_map/cond
  25.5 27.5 %copy-start.3 = (bf16[2,512,512]{2,1,0:T(8,128)(2,1)S(1)}, bf16[2,512,512]{2,1,0:T(8,128)(2,1)}, u32[]{:S(2)}) copy-start(bf16[2,512,512]{2,1,0:T(8,128)(2,1)} %get-tuple-element.32.right_ref) | copy-start | bytes 3145732 | tf_op jit(solution)/shard_map/cond
  54.8 24.9 %copy-start.5 = (bf16[32,8,512]{2,1,0:T(8,128)(2,1)S(1)}, bf16[32,8,512]{2,1,0:T(8,128)(2,1)}, u32[]{:S(2)}) copy-start(bf16[32,8,512]{2,1,0:T(8,128)(2,1)} %get-tuple-element.33.momentum_ref) | copy-start | bytes 786436 | tf_op jit(solution)/shard_map/cond
  80.4 3.9 %collective-permute-start.4 = (bf16[16,8,512]{2,1,0:T(8,128)(2,1)S(1)}, bf16[16,8,512]{2,1,0:T(8,128)(2,1)S(1)}, u32[]{:S(2)}, u32[]{:S(2)}) collective-permute-start(bf16[16,8,512]{2,1,0:T(8,128)(2,1)S(1)} %get-tuple-element.41.refs_0_), channel_id=1, source_target_pairs={{0,128},{64,192},{128,0},{192,64},{1,129},{65,193},{129,1},{193,65... | collective-permute-start | bytes 393224 | tf_op jit(solution)/shard_map/ppermute | solution.py:197
  80.8 4.9 %collective-permute-start.5 = (bf16[16,8,512]{2,1,0:T(8,128)(2,1)S(1)}, bf16[16,8,512]{2,1,0:T(8,128)(2,1)S(1)}, u32[]{:S(2)}, u32[]{:S(2)}) collective-permute-start(bf16[16,8,512]{2,1,0:T(8,128)(2,1)S(1)} %get-tuple-element.42.refs_1_), channel_id=1, source_target_pairs={{0,128},{64,192},{128,0},{192,64},{1,129},{65,193},{129,1},{193,65... | collective-permute-start | bytes 393224 | tf_op jit(solution)/shard_map/ppermute | solution.py:197
  82.0 3.8 %collective-permute-start.2 = (bf16[16,8,512]{2,1,0:T(8,128)(2,1)S(1)}, bf16[16,8,512]{2,1,0:T(8,128)(2,1)S(1)}, u32[]{:S(2)}, u32[]{:S(2)}) collective-permute-start(bf16[16,8,512]{2,1,0:T(8,128)(2,1)S(1)} %get-tuple-element.41.refs_0_), channel_id=1, source_target_pairs={{0,64},{64,0},{128,192},{192,128},{1,65},{65,1},{129,193},{193,129... | collective-permute-start | bytes 393224 | tf_op jit(solution)/shard_map/ppermute | solution.py:198
  82.0 3.8 %collective-permute-start.3 = (bf16[16,8,512]{2,1,0:T(8,128)(2,1)S(1)}, bf16[16,8,512]{2,1,0:T(8,128)(2,1)S(1)}, u32[]{:S(2)}, u32[]{:S(2)}) collective-permute-start(bf16[16,8,512]{2,1,0:T(8,128)(2,1)S(1)} %get-tuple-element.42.refs_1_), channel_id=1, source_target_pairs={{0,64},{64,0},{128,192},{192,128},{1,65},{65,1},{129,193},{193,129... | collective-permute-start | bytes 393224 | tf_op jit(solution)/shard_map/ppermute | solution.py:198
  84.4 1.4 %collective-permute-start.6 = (bf16[16,8,512]{2,1,0:T(8,128)(2,1)S(1)}, bf16[16,8,512]{2,1,0:T(8,128)(2,1)S(1)}, u32[]{:S(2)}, u32[]{:S(2)}) collective-permute-start(bf16[16,8,512]{2,1,0:T(8,128)(2,1)S(1)} %collective-permute-done.4.refs_4_), channel_id=1, source_target_pairs={{0,64},{64,0},{128,192},{192,128},{1,65},{65,1},{129,193},{193,129... | collective-permute-start | bytes 393224 | tf_op jit(solution)/shard_map/ppermute | solution.py:199
  85.8 1.3 %collective-permute-start.7 = (bf16[16,8,512]{2,1,0:T(8,128)(2,1)S(1)}, bf16[16,8,512]{2,1,0:T(8,128)(2,1)S(1)}, u32[]{:S(2)}, u32[]{:S(2)}) collective-permute-start(bf16[16,8,512]{2,1,0:T(8,128)(2,1)S(1)} %collective-permute-done.5.refs_5_), channel_id=1, source_target_pairs={{0,64},{64,0},{128,192},{192,128},{1,65},{65,1},{129,193},{193,129... | collective-permute-start | bytes 393224 | tf_op jit(solution)/shard_map/ppermute | solution.py:199

commit v4 on v3

--- a/solution.py
+++ b/solution.py
@@ -10,8 +10,8 @@
 momentum_decay = 0.9
 graft_eps = 1e-06
 LANES = 128
-HOPS = (36, 2)
-PIECES = (16, 16)
+HOPS = (20, 2)
+PIECES = (20, 12)
 
 
 def pack_kernel(owner_ref, grad_ref, out_ref, index_ref, count_ref):

time: 88.1 us -> 88.3 us (level)
  starting transfers between devices: 16.6 us -> 12.7 us
  waiting for transfers between devices: 11.2 us -> 13.4 us
  blocking collectives: 52.4 us -> 54.4 us
    ppermute x2, starting transfers between devices: 14.6 us -> 10.6 us  [late(): owners = lax.ppermute(owners, ('rep', 'shard'), hops)]
    ppermute x2, waiting for transfers between devices: 7.68 us -> 9.68 us  [late(): owners = lax.ppermute(owners, ('rep', 'shard'), hops)]
    all_to_all x2, blocking collectives: 52.4 us -> 54.4 us  [swap_rows(): return lax.all_to_all(rows, 'shard', 0, 0, tiled=True)]
where the time goes in v4:
time: 88.3 us; the launch traced here: 88 us
  blocking collectives  54.4 us (62%)
  waiting for transfers between devices  13.4 us (15%)
  starting transfers between devices  12.7 us (14%)
  Pallas kernels  6.15 us (7%)
    all_to_all x2, blocking collectives, swap_rows(): return lax.all_to_all(rows, 'shard', 0, 0, tiled=True)  54.4 us
    ppermute x2, starting transfers between devices, late(): owners = lax.ppermute(owners, ('rep', 'shard'), hops)  10.6 us
    ppermute x2, waiting for transfers between devices, late(): owners = lax.ppermute(owners, ('rep', 'shard'), hops)  9.68 us
    ppermute x2, waiting for transfers between devices, gather_parts(): chip = [lax.ppermute(piece, 'rep', swap_chip) for piece in own]  3.24 us
    pallas_call x1, Pallas kernels, pack(): pl.pallas_call(pack_kernel, out_shape=(jax.ShapeDtypeStruct((shard_count...  1.89 us
    pallas_call x1, Pallas kernels, precondition(): pl.pallas_call(precondition_kernel, out_shape=jax.ShapeDtypeStruct(arrive...  1.8 us
  transfers between devices with their start and end apart: 8, of which 5 were waited for; matrix products, arithmetic and copies ran while one was open for 0% of the time, Pallas kernels for 1%

profile of v4, /device:TPU:1, one launch (start us, length us, event | category | flops | bytes accessed | tf_op | source)
XLA Modules:
  0.0 88.0 jit_solution(1013876747295787711)
XLA Ops:
  0.6 0.0 copy-start.6
  0.6 0.6 copy-done.6
  1.3 79.2 %conditional.1 = ((bf16[32,8,512]{2,1,0:T(8,128)(2,1)S(1)}, bf16[20,8,512]{2,1,0:T(8,128)(2,1)S(1)}, bf16[12,8,512]{2,1,0:T(8,128)(2,1)S(1)})) conditional(s32[]{:T(128)} %convert_element_type.3, (s32[1,32]{1,0:T(1,128)S(1)}, f32[32,8,512]{2,1,0:T(8,128)}, bf16[2,512,512]{2,1,0:T(8,128)(2,1)}, bf16[2,512,512]{2,1,0:T(8,128)(2,1)}, ...), branch_computations={%region_0.0_spmd, %region_1.0_spmd} | conditional | bytes 13632684 | solution.py:239
  1.3 8.3 %collective-permute-start = (s32[1,32]{1,0:T(1,128)S(1)}, s32[1,32]{1,0:T(1,128)S(1)}, u32[]{:S(2)}, u32[]{:S(2)}) collective-permute-start(s32[1,32]{1,0:T(1,128)S(1)} %get-tuple-element.27), channel_id=1, source_target_pairs={{64,84},{65,85},{66,86},{67,87},{68,88},{69,89},{70,90},{71,91},{7... | collective-permute-start | bytes 392 | tf_op jit(solution)/shard_map/cond/branch_1_fun/ppermute | solution.py:233
  9.6 4.4 %collective-permute-done = s32[1,32]{1,0:T(1,128)S(1)} collective-permute-done((s32[1,32]{1,0:T(1,128)S(1)}, s32[1,32]{1,0:T(1,128)S(1)}, u32[]{:S(2)}, u32[]{:S(2)}) %collective-permute-start) | collective-permute-done | bytes 160 | tf_op jit(solution)/shard_map/cond/branch_1_fun/ppermute | solution.py:233
  14.0 2.3 %collective-permute-start.1 = (s32[1,32]{1,0:T(1,128)S(1)}, s32[1,32]{1,0:T(1,128)S(1)}, u32[]{:S(2)}, u32[]{:S(2)}) collective-permute-start(s32[1,32]{1,0:T(1,128)S(1)} %collective-permute-done), channel_id=1, source_target_pairs={{64,66},{65,67},{66,68},{67,69},{68,70},{69,71},{70,72},{71,73},{7... | collective-permute-start | bytes 392 | tf_op jit(solution)/shard_map/cond/branch_1_fun/ppermute | solution.py:233
  16.3 5.3 %collective-permute-done.1.owner_ref = s32[1,32]{1,0:T(1,128)S(1)} collective-permute-done((s32[1,32]{1,0:T(1,128)S(1)}, s32[1,32]{1,0:T(1,128)S(1)}, u32[]{:S(2)}, u32[]{:S(2)}) %collective-permute-start.1) | collective-permute-done | bytes 160 | tf_op jit(solution)/shard_map/cond/branch_1_fun/ppermute | solution.py:233
  21.6 1.9 %branch_1_fun.3 = (bf16[128,32,128]{2,1,0:T(8,128)(2,1)S(1)}, s32[32]{0:T(128)S(1)}) custom-call(s32[1,32]{1,0:T(1,128)S(1)} %collective-permute-done.1.owner_ref, f32[32,8,512]{2,1,0:T(8,128)} %get-tuple-element.28.grad_ref), custom_call_target="tpu_custom_call" | custom-call | tf_op jit(solution)/shard_map/cond/branch_1_fun/pallas_call | solution.py:47
  23.5 0.0 copy-start.1
  23.5 0.0 copy-start.3
  23.6 28.8 %all_to_all.18.arrived_ref = bf16[64,64,128]{2,1,0:T(8,128)(2,1)S(1)} all-to-all(bf16[64,64,128]{2,1,0:T(8,128)(2,1)S(1)} %bitcast.10), channel_id=1, replica_groups=mesh['rep'=4,'shard'=64] {'shard'}, dimensions={0} | all-to-all | bytes 2097152 | tf_op jit(solution)/shard_map/cond/branch_1_fun/all_to_all | solution.py:213
  52.3 0.0 copy-done.1
  52.4 0.0 copy-done.3
  52.4 1.8 %branch_1_fun.4 = bf16[64,64,128]{2,1,0:T(8,128)(2,1)S(1)} custom-call(bf16[64,64,128]{2,1,0:T(8,128)(2,1)S(1)} %all_to_all.18.arrived_ref, bf16[2,512,512]{2,1,0:T(8,128)(2,1)S(1)} %copy-done.1, bf16[2,512,512]{2,1,0:T(8,128)(2,1)S(1)} %copy-done.3), custom_call_target="tpu_custom_call" | custom-call | tf_op jit(solution)/shard_map/cond/branch_1_fun/pallas_call | solution.py:109
  54.2 0.0 copy-start.5
  54.2 25.6 %all_to_all.19 = bf16[64,64,128]{2,1,0:T(8,128)(2,1)S(1)} all-to-all(bf16[64,64,128]{2,1,0:T(8,128)(2,1)S(1)} %branch_1_fun.4), channel_id=1, replica_groups=mesh['rep'=4,'shard'=64] {'shard'}, dimensions={0} | all-to-all | bytes 2097152 | tf_op jit(solution)/shard_map/cond/branch_1_fun/all_to_all | solution.py:213
  79.8 0.0 copy-done.5
  79.8 0.7 branch_1_fun.5
  80.5 0.3 collective-permute-start.4
  80.8 1.2 %collective-permute-start.5 = (bf16[12,8,512]{2,1,0:T(8,128)(2,1)S(1)}, bf16[12,8,512]{2,1,0:T(8,128)(2,1)S(1)}, u32[]{:S(2)}, u32[]{:S(2)}) collective-permute-start(bf16[12,8,512]{2,1,0:T(8,128)(2,1)S(1)} %get-tuple-element.42.refs_1_), channel_id=1, source_target_pairs={{0,128},{64,192},{128,0},{192,64},{1,129},{65,193},{129,1},{193,65... | collective-permute-start | bytes 294920 | tf_op jit(solution)/shard_map/ppermute | solution.py:197
  82.0 0.0 collective-permute-start.2
  82.0 2.7 %collective-permute-done.4.refs_4_ = bf16[20,8,512]{2,1,0:T(8,128)(2,1)S(1)} collective-permute-done((bf16[20,8,512]{2,1,0:T(8,128)(2,1)S(1)}, bf16[20,8,512]{2,1,0:T(8,128)(2,1)S(1)}, u32[]{:S(2)}, u32[]{:S(2)}) %collective-permute-start.4) | collective-permute-done | bytes 163872 | tf_op jit(solution)/shard_map/ppermute | solution.py:197
  84.7 0.0 collective-permute-start.6
  84.7 0.5 collective-permute-start.3
  85.2 0.5 collective-permute-done.5.refs_5_
  85.8 0.0 collective-permute-start.7
  85.8 0.5 collective-permute-done.3.refs_3_
  86.3 0.0 collective-permute-done.2.refs_2_
  86.3 0.0 collective-permute-done.6.refs_6_
  86.3 1.1 %shard_map.68 = (bf16[4,32,8,512]{3,2,1,0:T(8,128)(2,1)}, bf16[32,8,512]{2,1,0:T(8,128)(2,1)}) custom-call(bf16[20,8,512]{2,1,0:T(8,128)(2,1)S(1)} %get-tuple-element.41.refs_0_, bf16[12,8,512]{2,1,0:T(8,128)(2,1)S(1)} %get-tuple-element.42.refs_1_, bf16[20,8,512]{2,1,0:T(8,128)(2,1)S(1)} %collective-permute-done.2.refs_2_, ...), custom_call_target="tpu_custom_call" | custom-call | tf_op jit(solution)/shard_map/pallas_call | solution.py:183
  87.4 0.0 collective-permute-done.7.refs_0_
  87.4 0.7 shard_map.69
Async XLA Ops:
  0.6 0.7 copy-start.6
  1.3 12.7 %collective-permute-start = (s32[1,32]{1,0:T(1,128)S(1)}, s32[1,32]{1,0:T(1,128)S(1)}, u32[]{:S(2)}, u32[]{:S(2)}) collective-permute-start(s32[1,32]{1,0:T(1,128)S(1)} %get-tuple-element.27), channel_id=1, source_target_pairs={{64,84},{65,85},{66,86},{67,87},{68,88},{69,89},{70,90},{71,91},{7... | collective-permute-start | bytes 392 | tf_op jit(solution)/shard_map/cond/branch_1_fun/ppermute | solution.py:233
  14.0 7.6 %collective-permute-start.1 = (s32[1,32]{1,0:T(1,128)S(1)}, s32[1,32]{1,0:T(1,128)S(1)}, u32[]{:S(2)}, u32[]{:S(2)}) collective-permute-start(s32[1,32]{1,0:T(1,128)S(1)} %collective-permute-done), channel_id=1, source_target_pairs={{64,66},{65,67},{66,68},{67,69},{68,70},{69,71},{70,72},{71,73},{7... | collective-permute-start | bytes 392 | tf_op jit(solution)/shard_map/cond/branch_1_fun/ppermute | solution.py:233
  23.5 28.8 %copy-start.1 = (bf16[2,512,512]{2,1,0:T(8,128)(2,1)S(1)}, bf16[2,512,512]{2,1,0:T(8,128)(2,1)}, u32[]{:S(2)}) copy-start(bf16[2,512,512]{2,1,0:T(8,128)(2,1)} %get-tuple-element.31.left_ref) | copy-start | bytes 3145732 | tf_op jit(solution)/shard_map/cond
  23.5 28.8 %copy-start.3 = (bf16[2,512,512]{2,1,0:T(8,128)(2,1)S(1)}, bf16[2,512,512]{2,1,0:T(8,128)(2,1)}, u32[]{:S(2)}) copy-start(bf16[2,512,512]{2,1,0:T(8,128)(2,1)} %get-tuple-element.32.right_ref) | copy-start | bytes 3145732 | tf_op jit(solution)/shard_map/cond
  54.2 25.6 %copy-start.5 = (bf16[32,8,512]{2,1,0:T(8,128)(2,1)S(1)}, bf16[32,8,512]{2,1,0:T(8,128)(2,1)}, u32[]{:S(2)}) copy-start(bf16[32,8,512]{2,1,0:T(8,128)(2,1)} %get-tuple-element.33.momentum_ref) | copy-start | bytes 786436 | tf_op jit(solution)/shard_map/cond
  80.5 4.3 %collective-permute-start.4 = (bf16[20,8,512]{2,1,0:T(8,128)(2,1)S(1)}, bf16[20,8,512]{2,1,0:T(8,128)(2,1)S(1)}, u32[]{:S(2)}, u32[]{:S(2)}) collective-permute-start(bf16[20,8,512]{2,1,0:T(8,128)(2,1)S(1)} %get-tuple-element.41.refs_0_), channel_id=1, source_target_pairs={{0,128},{64,192},{128,0},{192,64},{1,129},{65,193},{129,1},{193,65... | collective-permute-start | bytes 491528 | tf_op jit(solution)/shard_map/ppermute | solution.py:197
  80.8 5.0 %collective-permute-start.5 = (bf16[12,8,512]{2,1,0:T(8,128)(2,1)S(1)}, bf16[12,8,512]{2,1,0:T(8,128)(2,1)S(1)}, u32[]{:S(2)}, u32[]{:S(2)}) collective-permute-start(bf16[12,8,512]{2,1,0:T(8,128)(2,1)S(1)} %get-tuple-element.42.refs_1_), channel_id=1, source_target_pairs={{0,128},{64,192},{128,0},{192,64},{1,129},{65,193},{129,1},{193,65... | collective-permute-start | bytes 294920 | tf_op jit(solution)/shard_map/ppermute | solution.py:197
  82.0 4.2 %collective-permute-start.2 = (bf16[20,8,512]{2,1,0:T(8,128)(2,1)S(1)}, bf16[20,8,512]{2,1,0:T(8,128)(2,1)S(1)}, u32[]{:S(2)}, u32[]{:S(2)}) collective-permute-start(bf16[20,8,512]{2,1,0:T(8,128)(2,1)S(1)} %get-tuple-element.41.refs_0_), channel_id=1, source_target_pairs={{0,64},{64,0},{128,192},{192,128},{1,65},{65,1},{129,193},{193,129... | collective-permute-start | bytes 491528 | tf_op jit(solution)/shard_map/ppermute | solution.py:198
  84.7 1.5 %collective-permute-start.6 = (bf16[20,8,512]{2,1,0:T(8,128)(2,1)S(1)}, bf16[20,8,512]{2,1,0:T(8,128)(2,1)S(1)}, u32[]{:S(2)}, u32[]{:S(2)}) collective-permute-start(bf16[20,8,512]{2,1,0:T(8,128)(2,1)S(1)} %collective-permute-done.4.refs_4_), channel_id=1, source_target_pairs={{0,64},{64,0},{128,192},{192,128},{1,65},{65,1},{129,193},{193,129... | collective-permute-start | bytes 491528 | tf_op jit(solution)/shard_map/ppermute | solution.py:199
  84.7 1.5 %collective-permute-start.3 = (bf16[12,8,512]{2,1,0:T(8,128)(2,1)S(1)}, bf16[12,8,512]{2,1,0:T(8,128)(2,1)S(1)}, u32[]{:S(2)}, u32[]{:S(2)}) collective-permute-start(bf16[12,8,512]{2,1,0:T(8,128)(2,1)S(1)} %get-tuple-element.42.refs_1_), channel_id=1, source_target_pairs={{0,64},{64,0},{128,192},{192,128},{1,65},{65,1},{129,193},{193,129... | collective-permute-start | bytes 294920 | tf_op jit(solution)/shard_map/ppermute | solution.py:198
  85.8 1.6 %collective-permute-start.7 = (bf16[12,8,512]{2,1,0:T(8,128)(2,1)S(1)}, bf16[12,8,512]{2,1,0:T(8,128)(2,1)S(1)}, u32[]{:S(2)}, u32[]{:S(2)}) collective-permute-start(bf16[12,8,512]{2,1,0:T(8,128)(2,1)S(1)} %collective-permute-done.5.refs_5_), channel_id=1, source_target_pairs={{0,64},{64,0},{128,192},{192,128},{1,65},{65,1},{129,193},{193,129... | collective-permute-start | bytes 294920 | tf_op jit(solution)/shard_map/ppermute | solution.py:199
